TPU v7x, 256 devices: a whole 4x4x8 slice. The times are simulated.
256 devices in a mesh: space: 32 (over z_hi, y, core), rot: 8 (over z_lo, x).
Axes of the slice: x: 4, y: 4, z: 8 (z_hi: 4, z_lo: 2; z = z_hi * 2 + z_lo), core: 2. Of those that a mesh axis runs over, the one named last changes fastest.
Arguments:
- features: bfloat16 [24, 16, 32, 8, 128], P('rot', None, 'space'), may hold values from -6 to 6
- cotangent: bfloat16 [24, 16, 32, 8, 128], P('rot', None, 'space'), may hold values from -6 to 6
- weight: bfloat16 [27, 24, 256], replicated, may hold values from -0.0625 to 0.0625
- relative: int32 [24, 24], replicated, may hold values from 0 to 23, as said below
- offset_perm: int32 [24, 27], replicated, may hold values from 0 to 26, as said below
Outputs:
- feature_grad: bfloat16 [24, 16, 32, 8, 128], P('rot', None, 'space')
- weight_grad: float32 [27, 24, 256], replicated
Inputs may be any that keep to these rules, and one draw needn't show every extreme that they name: relative[h, g] is the label of the inverse of rotation h composed with rotation g, for the 24 rotations of the cube under one labelling that is drawn afresh; every row and every column is a permutation. offset_perm[h, q] is the index of the offset obtained by applying the inverse of rotation h, as a 3 x 3 signed permutation matrix on (first, second, third) spatial offsets, to offset q; it uses the labelling of relative; every row is a permutation.
All inputs are finite; a program needn't handle non-finite values.
Results may differ from a plain program's by a relative error of at most 0.001.
Values may be sent and summed in bfloat16 or wider, within the bound.
A program may use at most 384 MiB of HBM per device.

v0:
```python
import math

import jax
import jax.numpy as jnp
from jax import lax
from jax.sharding import PartitionSpec as P


def with_halo(cells, sides, width):
    for axis, dim in sides:
        count = lax.axis_size(axis)
        ends = count - 1
        head = lax.slice_in_dim(cells, 0, width, axis=dim)
        tail = lax.slice_in_dim(cells, cells.shape[dim] - width, cells.shape[dim], axis=dim)
        cells = jnp.concatenate(
            [
                lax.ppermute(tail, axis, [(i, (i + 1) % count) for i in range(ends)]),
                cells,
                lax.ppermute(head, axis, [((i + 1) % count, i) for i in range(ends)]),
            ],
            axis=dim,
        )
    return cells


def tap_offsets():
    return [
        (tap_index // 9 - 1, tap_index // 3 % 3 - 1, tap_index % 3 - 1) for tap_index in range(27)
    ]


def shift_axis(values, amount, along_axis):
    if amount == 0:
        return values
    length = values.shape[along_axis]
    zero_shape = list(values.shape)
    zero_shape[along_axis] = 1
    zero_plane = jnp.zeros(zero_shape, values.dtype)
    if amount > 0:
        kept_part = lax.slice_in_dim(values, 0, length - 1, axis=along_axis)
        return jnp.concatenate([zero_plane, kept_part], along_axis)
    kept_part = lax.slice_in_dim(values, 1, length, axis=along_axis)
    return jnp.concatenate([kept_part, zero_plane], along_axis)


def gather_taps(haloed, slab_depth):
    stacked = []
    for tap_z, tap_y, tap_x in tap_offsets():
        slab_part = lax.slice_in_dim(haloed, 1 - tap_z, 1 - tap_z + slab_depth, axis=2)
        slab_part = shift_axis(shift_axis(slab_part, tap_y, 3), tap_x, 4)
        stacked.append(slab_part.reshape(slab_part.shape[0], slab_part.shape[1], -1))
    return jnp.stack(stacked, 0)


def label_hot(relative, h_first, h_count, g_count):
    window = lax.dynamic_slice(relative, (h_first, 0), (h_count, g_count))
    labels = jnp.arange(relative.shape[0], dtype=jnp.int32)
    return (window[:, :, None] == labels[None, None, :]).astype(jnp.float32)


def tap_hot(offset_perm, h_first, h_count):
    window = lax.dynamic_slice_in_dim(offset_perm, h_first, h_count, 0)
    labels = jnp.arange(offset_perm.shape[1], dtype=jnp.int32)
    return (window[:, :, None] == labels[None, None, :]).astype(jnp.float32)


def input_terms(weight_full, label_table, tap_table, tap_stack):
    per_tap = jnp.einsum("hoq,qkcj->ohkcj", tap_table, weight_full, precision=lax.Precision.HIGHEST)
    turned = jnp.einsum("hgk,ohkcj->ohgcj", label_table, per_tap, precision=lax.Precision.HIGHEST)
    turned = turned.astype(jnp.bfloat16)
    return jnp.einsum("ohgcj,ohcp->gjp", turned, tap_stack, preferred_element_type=jnp.float32)


def weight_terms(tap_stack, flat_features, label_table, tap_table):
    pair_sums = jnp.einsum(
        "ohcp,gjp->ohcgj", tap_stack, flat_features, preferred_element_type=jnp.float32
    )
    by_label = jnp.einsum(
        "hgk,ohcgj->ohkcj", label_table, pair_sums, precision=lax.Precision.HIGHEST
    )
    return jnp.einsum("hoq,ohkcj->qkcj", tap_table, by_label, precision=lax.Precision.HIGHEST)


def local(features, cotangent, weight, relative, offset_perm):
    local_rots, channels, slab_depth, height, row_width = features.shape
    group_order = relative.shape[0]
    rot_first = lax.axis_index("rot") * local_rots
    weight_full = weight.astype(jnp.float32).reshape(
        weight.shape[0], group_order, channels, channels
    )
    haloed = with_halo(cotangent, (("space", 2),), 1)
    tap_stack = gather_taps(haloed, slab_depth)
    tap_table = tap_hot(offset_perm, rot_first, local_rots)
    shard_piece = lax.all_gather(features, "rot", axis=0, tiled=True)
    row_count = shard_piece.shape[0]
    label_table = label_hot(relative, rot_first, local_rots, row_count)
    piece_flat = shard_piece.reshape(row_count, channels, -1)
    weight_local = weight_terms(tap_stack, piece_flat, label_table, tap_table)
    label_table = label_hot(relative, rot_first, local_rots, local_rots * lax.axis_size("rot"))
    input_grad = lax.psum_scatter(
        input_terms(weight_full, label_table, tap_table, tap_stack),
        "rot",
        scatter_dimension=0,
        tiled=True,
    )
    feature_grad = input_grad.reshape(features.shape).astype(jnp.bfloat16)
    weight_total = lax.psum(weight_local, ("space", "rot"))
    voxel_count = slab_depth * lax.axis_size("space") * height * row_width
    weight_grad = (weight_total / math.sqrt(group_order * voxel_count)).reshape(weight.shape)
    return (feature_grad, weight_grad)


def solution(mesh):
    placed = (
        P("rot", None, "space", None, None),
        P("rot", None, "space", None, None),
        P(),
        P(),
        P(),
    )
    return jax.shard_map(
        local,
        mesh=mesh,
        in_specs=placed,
        out_specs=(P("rot", None, "space", None, None), P()),
        check_vma=False,
    )
```

profile of v0, /device:TPU:1, one launch (start us, length us, event | category | flops | bytes accessed | tf_op | source)
XLA Modules:
  0.0 420.2 jit_solution(6985913036311195596)
XLA Ops:
  8.1 5.2 %collective-permute-start = (bf16[3,16,1,8,128]{4,3,2,1,0:T(8,128)(2,1)}, bf16[3,16,1,8,128]{4,3,2,1,0:T(8,128)(2,1)S(1)}, u32[]{:S(2)}, u32[]{:S(2)}) collective-permute-start(bf16[3,16,1,8,128]{4,3,2,1,0:T(8,128)(2,1)} %param.6), channel_id=1, source_target_pairs={{8,0},{16,8},{24,16},{32,24},{40,32},{48,40},{56,48},{64,56},{72,6... | collective-permute-start | bytes 294920 | tf_op jit(solution)/shard_map/ppermute | solution.py:19
  13.2 1.9 collective-permute-start.1
  15.2 0.9 stack_reshape.94
  16.1 1.1 fusion.32
  17.2 1.0 fusion.31
  18.2 1.2 constant_dynamic-slice_fusion
  20.5 0.8 copy.77
  21.4 25.1 %all_gather.3 = bf16[24,16,1,8,128]{4,3,2,1,0:T(8,128)(2,1)S(1)} all-gather(bf16[3,16,1,8,128]{4,3,2,1,0:T(8,128)(2,1)} %param.5), channel_id=1, replica_groups=mesh['space'=32,'rot'=8] {'rot'}, dimensions={0}, use_global_device_ids=true | all-gather | bytes 884736 | tf_op jit(solution)/shard_map/all_gather | solution.py:94
  46.4 1.9 copy.111
  48.4 1.9 fusion.18
  50.2 6.5 %convert_bitcast_fusion = bf16[27,3,24,16,16]{0,2,4,3,1:T(8,128)(2,1)} fusion(f32[3,27,24,16,16]{1,2,4,3,0:T(8,128)S(1)} %fusion.18, s32[3,24]{1,0:T(4,128)S(1)} %copy-done.3), kind=kOutput, calls=%fused_computation.6 | convolution fusion | flops 143826624 | bytes 2986272 | tf_op jit(solution)/shard_map/hgk,ohkcj->ohgcj/dot_general | solution.py:69
  58.0 1.3 reshape.41
  59.4 0.8 pad_slice_fusion
  61.6 0.8 pad_slice_fusion.8
  65.0 1.0 copy.91
  66.0 1.5 concatenate.101
  67.6 1.6 stack_reshape.99
  69.2 1.7 copy.85
  70.9 1.6 concatenate.102
  72.6 1.6 stack_reshape.101
  74.1 1.7 copy.87
  75.9 1.6 stack_reshape.88
  77.4 1.7 copy.74
  79.1 1.6 stack_reshape.82
  80.7 1.7 copy.68
  82.5 0.7 fusion.34
  83.3 0.7 stack_reshape.86
  84.0 1.7 copy.72
  85.7 0.9 concatenate.87
  87.3 1.7 copy.70
  89.1 1.0 concatenate.91
  90.0 0.7 stack_reshape.89
  90.7 1.7 copy.75
  92.4 0.9 concatenate.90
  94.1 1.7 copy.73
  95.8 0.9 concatenate.85
  97.4 1.7 copy.67
  99.2 0.9 copy.69
  100.1 17.4 %stack.3 = bf16[27,3,16,1024]{3,0,1,2:T(8,128)(2,1)} concatenate(bf16[1,3,16,1024]{3,0,1,2:T(2,128)(2,1)} %copy.67, bf16[1,3,16,1024]{3,0,1,2:T(2,128)(2,1)} %copy.68, bf16[1,3,16,1024]{3,0,1,2:T(2,128)(2,1)} %copy.69, bf16[1,3,16,1024]{3,0,1,2:T(2,128)(2,1)} %copy.70, bf16[1,3,16,1024]{3,0,1,2:T(2,128)(2,1)S(1)} %copy.71, bf16[1,3,16,1024]{3,0,1,2:T(2,128)(2,1)} %copy.72, ...), dimensions={0} | concatenate | bytes 5308416 | tf_op jit(solution)/shard_map/stack | solution.py:52
  117.5 7.3 %fusion.6 = f32[27,3,16,24,16]{0,3,1,4,2:T(8,128)S(1)} fusion(bf16[27,3,16,1024]{3,0,1,2:T(8,128)(2,1)} %stack.3, bf16[24,16,1024,1,1]{2,1,0,4,3:T(8,128)(2,1)} %bitcast.120), kind=kOutput, calls=%fused_computation.7 | convolution fusion | flops 1019215872 | bytes 5431296 | tf_op jit(solution)/shard_map/ohcp,gjp->ohcgj/dot_general | solution.py:75
  124.7 5.2 %fusion.23 = f32[3,27,16,16,24]{1,4,0,3,2:T(8,128)S(1)} fusion(f32[27,3,16,24,16]{0,3,1,4,2:T(8,128)S(1)} %fusion.6, s32[3,24]{1,0:T(4,128)S(1)} %copy-done.4), kind=kOutput, calls=%fused_computation.21 | convolution fusion | flops 143328960 | bytes 3981600 | tf_op jit(solution)/shard_map/hgk,ohcgj->ohkcj/dot_general | solution.py:78
  130.0 7.3 %fusion.11 = f32[27,24,16,16]{0,1,3,2:T(8,128)} fusion(f32[3,27,16,16,24]{1,4,0,3,2:T(8,128)S(1)} %fusion.23, s32[3,27]{1,0:T(4,128)S(1)} %constant_dynamic-slice_fusion.1), kind=kOutput, calls=%fused_computation.10 | convolution fusion | flops 161245328 | bytes 2654532 | tf_op jit(solution)/shard_map/hoq,ohkcj->qkcj/dot_general | solution.py:81
  137.4 5.7 %fusion.4 = f32[24,16,1024,1,1]{2,0,1,4,3:T(8,128)S(1)} fusion(bf16[27,3,24,16,16]{0,2,4,3,1:T(8,128)(2,1)} %convert_bitcast_fusion, bf16[27,3,16,1024]{3,0,1,2:T(8,128)(2,1)S(1)} %copy-done.1), kind=kOutput, calls=%fused_computation.4 | convolution fusion | flops 1019215872 | bytes 5222400 | tf_op jit(solution)/shard_map/ohgcj,ohcp->gjp/dot_general | solution.py:71
  143.1 2.1 copy.126
  145.2 261.8 %all-reduce.26.cloned.1.call-done = f32[27,24,16,16]{0,1,3,2:T(8,128)} async-done(((f32[27,24,16,16]{0,1,3,2:T(8,128)}), f32[27,24,16,16]{0,1,3,2:T(8,128)}) %all-reduce.26.cloned.1.call-update) | async-done | bytes 663568 | tf_op jit(solution)/shard_map/psum | solution.py:107
  407.0 2.2 broadcast_multiply_fusion
  409.2 1.9 copy.99
  411.1 0.9 convert_element_type.26
  (76 shorter events, 9.2 us)
Async XLA Ops:
  8.0 11.4 %copy-start = (s32[24,27]{1,0:T(8,128)S(1)}, s32[24,27]{1,0:T(8,128)}, u32[]{:S(2)}) copy-start(s32[24,27]{1,0:T(8,128)} %param.9) | copy-start | bytes 7780
  8.0 399.0 %all-reduce.26.cloned.1.call-start = ((), (), s32[]{:S(2)}) async-start(), calls=%async_computation.2 | async-start | bytes 6291456 | tf_op jit(solution)/shard_map/psum | solution.py:107
  8.1 52.2 %collective-permute-start = (bf16[3,16,1,8,128]{4,3,2,1,0:T(8,128)(2,1)}, bf16[3,16,1,8,128]{4,3,2,1,0:T(8,128)(2,1)S(1)}, u32[]{:S(2)}, u32[]{:S(2)}) collective-permute-start(bf16[3,16,1,8,128]{4,3,2,1,0:T(8,128)(2,1)} %param.6), channel_id=1, source_target_pairs={{8,0},{16,8},{24,16},{32,24},{40,32},{48,40},{56,48},{64,56},{72,6... | collective-permute-start | bytes 294920 | tf_op jit(solution)/shard_map/ppermute | solution.py:19
  13.2 46.1 %collective-permute-start.1 = (bf16[3,16,1,8,128]{4,3,2,1,0:T(8,128)(2,1)}, bf16[3,16,1,8,128]{4,3,2,1,0:T(8,128)(2,1)S(1)}, u32[]{:S(2)}, u32[]{:S(2)}) collective-permute-start(bf16[3,16,1,8,128]{4,3,2,1,0:T(8,128)(2,1)} %param.6), channel_id=1, source_target_pairs={{0,8},{8,16},{16,24},{24,32},{32,40},{40,48},{48,56},{56,64},{64,7... | collective-permute-start | bytes 294920 | tf_op jit(solution)/shard_map/ppermute | solution.py:17
  48.3 1.9 copy-start.3
  63.5 36.6 %copy-start.2 = (bf16[1,3,16,1024]{3,0,1,2:T(2,128)(2,1)S(1)}, bf16[1,3,16,1024]{3,0,1,2:T(2,128)(2,1)}, u32[]{:S(2)}) copy-start(bf16[1,3,16,1024]{3,0,1,2:T(2,128)(2,1)} %copy.77) | copy-start | bytes 294916
  117.5 7.3 %copy-start.4 = (s32[3,24]{1,0:T(4,128)S(1)}, s32[3,24]{1,0:T(4,128)}, u32[]{:S(2)}) copy-start(s32[3,24]{1,0:T(4,128)} %constant_dynamic-slice_fusion) | copy-start | bytes 868
  130.0 7.4 %copy-start.1 = (bf16[27,3,16,1024]{3,0,1,2:T(8,128)(2,1)S(1)}, bf16[27,3,16,1024]{3,0,1,2:T(8,128)(2,1)}, u32[]{:S(2)}) copy-start(bf16[27,3,16,1024]{3,0,1,2:T(8,128)(2,1)} %stack.3) | copy-start | bytes 7962628
  137.3 273.8 %reduce-scatter.2.cloned.1.call-start = ((), (), s32[]{:S(2)}) async-start(), calls=%async_computation.1 | async-start | bytes 1769472 | tf_op jit(solution)/shard_map/reduce_scatter | solution.py:100
Sparse Core Ops, SparseCore 0:
  137.4 269.5 all-reduce.25
Sparse Core Ops, SparseCore 1:
  145.3 44.5 reduce-scatter.1
where the time goes:
time: 423 us; the launch traced here: 420 us
  waiting for transfers between devices  262 us (62%)
  local copies, waits for them, and re-layouts  73.1 us (17%)
  matrix products  33.8 us (8%)
  blocking collectives  25.1 us (6%)
  between operations  16 us (4%)
  starting transfers between devices  7.16 us (2%)
    psum x1, waiting for transfers between devices, local(): weight_total = lax.psum(weight_local, ('space', 'rot'))  262 us
    another operation x55, local copies, waits for them, and re-layouts, gather_taps(): return jnp.stack(stacked, 0)  50 us
    all_gather x1, blocking collectives, local(): shard_piece = lax.all_gather(features, 'rot', axis=0, tiled=True)  25.1 us
  transfers between devices with their start and end apart: 4, of which 1 were waited for; matrix products, arithmetic and copies ran while one was open for 8% of the time, Pallas kernels for 0%

commit v1 on v0

v1 whole, which is shorter than its diff:
```python
import functools
import math

import jax
import jax.numpy as jnp
from jax import lax
from jax.experimental import pallas as pl
from jax.experimental.pallas import tpu as pltpu
from jax.sharding import PartitionSpec as P

MESH = pl.DeviceIdType.MESH
F32 = jnp.float32
BF16 = jnp.bfloat16
G, C, TAPS, Y, X = 24, 16, 27, 8, 128
ROT, SPACE = 8, 32
LOCAL = G // ROT
ROWS = LOCAL * C
VOX = Y * X
HALF = 14
UNIT = 48


def lane_iota(rows):
    return lax.broadcasted_iota(jnp.int32, (rows, X), 1)


def kernel(rel, perm, cot_in, feat_in, w_in, fg_out, wg_out,
           stage, win, lay, cot, feats, f27, pc, w32, wsrc32, wsrc, wmat, quad, table,
           summed, core_in, xy_in, z_in, unit, trans, fgm, part, part_in,
           in_sem, rot_send, rot_recv, halo_send, halo_recv, core_send, core_recv,
           xy_send, xy_recv, z_send, z_recv, ag_send, ag_recv, fwd_send, fwd_recv,
           pt_send, pt_recv):
    s = lax.axis_index("space")
    r = lax.axis_index("rot")
    core = lax.rem(s, 2)
    yy = lax.rem(s // 2, 4)
    z_hi = s // 8
    xx = lax.rem(r, 4)
    z_lo = r // 4
    m = yy * 4 + xx
    zz = z_hi * 2 + z_lo
    up, down = lax.rem(s + 1, SPACE), lax.rem(s + SPACE - 1, SPACE)
    sibling = s + 1 - 2 * core

    def xy_dev(i):
        return ((z_hi * 4 + i // 4) * 2 + core, z_lo * 4 + lax.rem(i, 4))

    def z_dev(i):
        return (((i // 2) * 4 + yy) * 2 + core, lax.rem(i, 2) * 4 + xx)

    cot_copy = pltpu.make_async_copy(cot_in, stage.at[0], in_sem.at[0])
    feat_copy = pltpu.make_async_copy(feat_in, stage.at[1], in_sem.at[1])
    w_copy = pltpu.make_async_copy(w_in, win, in_sem.at[2])
    cot_copy.start()
    feat_copy.start()
    w_copy.start()
    barrier = pltpu.get_barrier_semaphore()
    for d in range(1, ROT):
        pl.semaphore_signal(barrier, inc=1, device_id=(s, lax.rem(r + d, ROT)), device_id_type=MESH)
        pl.semaphore_signal(barrier, inc=1, device_id=z_dev(lax.rem(zz + d, 8)), device_id_type=MESH)
    for d in range(1, 16):
        pl.semaphore_signal(barrier, inc=1, device_id=xy_dev(lax.rem(m + d, 16)), device_id_type=MESH)
    for other in (up, down):
        pl.semaphore_signal(barrier, inc=1, device_id=(other, r), device_id_type=MESH)

    def flatten_plane(index, dst, row):
        lay[...] = stage[index].astype(F32).reshape(ROWS * Y, X)
        for y in range(Y):
            column = lay[pl.ds(y, ROWS, stride=Y), :].astype(BF16)
            dst[pl.ds(row, LOCAL), :, y * X:(y + 1) * X] = column.reshape(LOCAL, C, X)

    own = r * LOCAL
    cot_copy.wait()
    flatten_plane(0, cot, own)
    feat_copy.wait()
    flatten_plane(1, feats, LOCAL)
    pl.semaphore_wait(barrier, 31)

    def rot_copy(d):
        peer = lax.rem(r + d, ROT)
        return pltpu.make_async_remote_copy(
            src_ref=cot.at[pl.ds(own, LOCAL)], dst_ref=cot.at[pl.ds(own, LOCAL)],
            send_sem=rot_send.at[d], recv_sem=rot_recv.at[r],
            device_id=(s, peer), device_id_type=MESH)

    def rot_arrival(d):
        peer = lax.rem(r + d, ROT)
        block = cot.at[pl.ds(peer * LOCAL, LOCAL)]
        return pltpu.make_async_remote_copy(
            src_ref=block, dst_ref=block, send_sem=rot_send.at[d], recv_sem=rot_recv.at[peer],
            device_id=(s, peer), device_id_type=MESH)

    def halo_copy(side):
        return pltpu.make_async_remote_copy(
            src_ref=feats.at[pl.ds(LOCAL, LOCAL)], dst_ref=feats.at[pl.ds(2 * LOCAL * side, LOCAL)],
            send_sem=halo_send.at[side], recv_sem=halo_recv.at[side],
            device_id=(up if side == 0 else down, r), device_id_type=MESH)

    for d in range(1, ROT):
        rot_copy(d).start()
    for side in range(2):
        halo_copy(side).start()

    same = rel[0, 0]

    def fill_table(step, carry):
        g, k = step // G, lax.rem(step, G)
        h = rel[rel[r * LOCAL + g, same], rel[k, same]]
        turned_back = rel[h, same]
        table[step, 28] = h
        for q in range(TAPS):
            table[step, q] = perm[turned_back, q]
        table[step, TAPS] = 0
        return carry

    lax.fori_loop(0, LOCAL * G, fill_table, 0)

    w_copy.wait()

    def widen(q, carry):
        w32[pl.ds(pl.multiple_of(q * G, 8), G), :] = win[q].astype(F32)
        return carry

    lax.fori_loop(0, TAPS, widen, 0)
    row_id = lax.broadcasted_iota(jnp.int32, (C * C, 2 * X), 0)
    col_id = lax.broadcasted_iota(jnp.int32, (C * C, 2 * X), 1)

    def spread(step, carry):
        hot = jnp.logical_and(row_id // C == lax.rem(col_id, C), lax.rem(row_id, C) == 2 * step + col_id // X)
        picked = jnp.dot(w32[...].astype(BF16), hot.astype(F32).astype(BF16), preferred_element_type=F32)
        for side in range(2):
            wsrc32[pl.ds(2 * step + side, TAPS * G, stride=C), :] = picked[:, side * X:(side + 1) * X]
        return carry

    lax.fori_loop(0, C // 2, spread, 0)

    def narrow(step, carry):
        rows = pl.ds(pl.multiple_of(step * G * C, 16), G * C)
        wsrc[pl.ds(step * G, G)] = wsrc32[rows, :].astype(BF16).reshape(G, C, X)
        return carry

    lax.fori_loop(0, TAPS, narrow, 0)
    group16 = lane_iota(C) // C

    def fill_filter(step, carry):
        o, g = step // LOCAL, lax.rem(step, LOCAL)
        for octet in range(3):
            merged = None
            for j in range(8):
                h = octet * 8 + j
                block = wsrc[perm[h, o] * G + rel[h, r * LOCAL + g]]
                merged = block if merged is None else jnp.where(group16 == j, block, merged)
            wmat[pl.ds(pl.multiple_of(step * C, 16), C), octet * X:(octet + 1) * X] = merged
        return carry

    lax.fori_loop(0, TAPS * LOCAL, fill_filter, 0)

    for side in range(2):
        halo_copy(side).wait_recv()
    lane48 = lane_iota(ROWS)

    def fill_shifts(a, carry):
        inside = jnp.logical_and(jnp.logical_or(a != 0, s != 0), jnp.logical_or(a != 2, s != SPACE - 1))
        keep = jnp.where(inside, 1.0, 0.0).astype(F32)
        blank = jnp.zeros((C, X), BF16)
        for y in range(Y):
            plane = feats[pl.ds(a * LOCAL, LOCAL), :, y * X:(y + 1) * X].astype(F32).reshape(ROWS, X) * keep
            for c in range(3):
                if c == 0:
                    moved = jnp.where(lane48 == 0, 0.0, pltpu.roll(plane, 1, 1))
                elif c == 2:
                    moved = jnp.where(lane48 == X - 1, 0.0, pltpu.roll(plane, X - 1, 1))
                else:
                    moved = plane
                moved = moved.astype(BF16)
                for b in range(3):
                    target = y - (b - 1)
                    at = pl.multiple_of((a * 9 + b * 3 + c) * C, 16)
                    for g in range(LOCAL):
                        if 0 <= target < Y:
                            f27[g, pl.ds(at, C), target * X:(target + 1) * X] = moved[g * C:(g + 1) * C]
                        if (b == 2 and y == Y - 1) or (b == 0 and y == 0):
                            f27[g, pl.ds(at, C), y * X:(y + 1) * X] = blank
        return carry

    lax.fori_loop(0, 3, fill_shifts, 0)

    for d in range(1, ROT):
        rot_arrival(d).wait_recv()

    def reorder(step, carry):
        g, k = step // G, lax.rem(step, G)
        pc[g, pl.ds(pl.multiple_of(k * C, 16), C), :] = cot[table[step, 28]]
        return carry

    lax.fori_loop(0, LOCAL * G, reorder, 0)

    def pair_sums(g, carry):
        product = lax.dot_general(f27[g], pc[g], (((1,), (1,)), ((), ())), preferred_element_type=F32)
        quad[g] = product.reshape(TAPS, C, G * C)
        return carry

    lax.fori_loop(0, LOCAL, pair_sums, 0)

    def relabel(q, carry):
        for octet in range(3):
            total = None
            for g in range(LOCAL):
                merged = None
                for j in range(8):
                    block = quad[g, table[g * G + octet * 8 + j, q], :, octet * X:(octet + 1) * X]
                    merged = block if merged is None else jnp.where(group16 == j, block, merged)
                total = merged if total is None else total + merged
            summed[q, octet * C:(octet + 1) * C, :] = total
        return carry

    mine = core * HALF
    theirs = HALF - mine
    lax.fori_loop(theirs, theirs + HALF, relabel, 0)
    core_copy = pltpu.make_async_remote_copy(
        src_ref=summed.at[pl.ds(theirs, HALF)], dst_ref=core_in, send_sem=core_send, recv_sem=core_recv,
        device_id=(sibling, r), device_id_type=MESH)
    core_copy.start()
    lax.fori_loop(mine, mine + HALF, relabel, 0)
    core_copy.wait_recv()

    def xy_copy(i):
        return pltpu.make_async_remote_copy(
            src_ref=summed.at[mine + i], dst_ref=xy_in.at[m], send_sem=xy_send.at[i], recv_sem=xy_recv.at[m],
            device_id=xy_dev(i), device_id_type=MESH)

    for i in range(HALF):
        summed[mine + i] += core_in[i]

        @pl.when(m != i)
        def _():
            xy_copy(i).start()

    def input_part(a):
        def product(n, carry):
            cols = pl.ds(pl.multiple_of(n * 256, 256), 256)
            fgm[:, cols] = jnp.dot(
                wmat[a * 9 * ROWS:(a + 1) * 9 * ROWS, :], cot[:, :, cols].reshape(G * C, 256), preferred_element_type=F32)
            return carry

        lax.fori_loop(0, VOX // 256, product, 0)
        for y in range(Y):
            total = None
            for c in range(3):
                column = None
                for b in range(3):
                    source = y - (b - 1)
                    if 0 <= source < Y:
                        term = fgm[(b * 3 + c) * ROWS:(b * 3 + c + 1) * ROWS, source * X:(source + 1) * X]
                        column = term if column is None else column + term
                if c == 0:
                    column = jnp.where(lane48 == X - 1, 0.0, pltpu.roll(column, X - 1, 1))
                elif c == 2:
                    column = jnp.where(lane48 == 0, 0.0, pltpu.roll(column, 1, 1))
                total = column if total is None else total + column
            part[a, :, y * X:(y + 1) * X] = total

    def part_copy(side):
        return pltpu.make_async_remote_copy(
            src_ref=part.at[2 - 2 * side], dst_ref=part_in.at[side], send_sem=pt_send.at[side],
            recv_sem=pt_recv.at[side], device_id=(up if side == 0 else down, r), device_id_type=MESH)

    input_part(2)
    part_copy(0).start()
    input_part(0)
    part_copy(1).start()

    def z_copy(d):
        peer = lax.rem(zz + d, 8)
        return pltpu.make_async_remote_copy(
            src_ref=unit, dst_ref=z_in.at[zz], send_sem=z_send.at[d], recv_sem=z_recv.at[zz],
            device_id=z_dev(peer), device_id_type=MESH)

    @pl.when(m < HALF)
    def _():
        unit[...] = summed[mine + m]
        for d in range(1, 16):
            peer = lax.rem(m + d, 16)
            pltpu.make_async_remote_copy(
                src_ref=summed.at[0], dst_ref=xy_in.at[peer], send_sem=xy_send.at[0], recv_sem=xy_recv.at[peer],
                device_id=xy_dev(peer), device_id_type=MESH).wait_recv()
            unit[...] += xy_in[peer]
        z_in[zz] = unit[...]
        for d in range(1, 8):
            z_copy(d).start()

    input_part(1)

    def ag_copy(d):
        peer = lax.rem(m + d, 16)
        return pltpu.make_async_remote_copy(
            src_ref=wg_out.at[mine + m], dst_ref=wg_out.at[mine + m], send_sem=ag_send.at[d], recv_sem=ag_recv.at[m],
            device_id=xy_dev(peer), device_id_type=MESH)

    def forward(i):
        return pltpu.make_async_remote_copy(
            src_ref=wg_out.at[mine + i], dst_ref=wg_out.at[mine + i], send_sem=fwd_send.at[i], recv_sem=fwd_recv.at[i],
            device_id=(sibling, r), device_id_type=MESH)

    @pl.when(m < HALF)
    def _():
        for d in range(1, 8):
            peer = lax.rem(zz + d, 8)
            pltpu.make_async_remote_copy(
                src_ref=unit, dst_ref=z_in.at[peer], send_sem=z_send.at[d], recv_sem=z_recv.at[peer],
                device_id=z_dev(peer), device_id_type=MESH).wait_recv()
        total = z_in[0]
        for i in range(1, 8):
            total = total + z_in[i]
        total = total * (1.0 / math.sqrt(G * SPACE * VOX))
        blank = jnp.zeros((X - C, X), F32)
        for octet in range(3):
            trans[...] = jnp.concatenate([total[octet * C:(octet + 1) * C], blank], 0).T
            for side in range(2):
                joined = None
                for j in range(8):
                    rows = trans[pl.ds(side * 8 + j, 8, stride=C), :]
                    rows = rows if j == 0 else pltpu.roll(rows, j * C, 1)
                    joined = rows if joined is None else joined + rows
                wg_out[mine + m, octet * 8:(octet + 1) * 8, side * X:(side + 1) * X] = joined
        for d in range(1, 16):
            ag_copy(d).start()
        forward(m).start()

    for side in range(2):
        part_copy(side).wait_recv()
    low = jnp.where(s > 0, 1.0, 0.0).astype(F32)
    high = jnp.where(s < SPACE - 1, 1.0, 0.0).astype(F32)
    for y in range(Y):
        cols = slice(y * X, (y + 1) * X)
        lay[pl.ds(y, ROWS, stride=Y), :] = part[1, :, cols] + low * part_in[0, :, cols] + high * part_in[1, :, cols]
    fg_out[...] = lay[...].reshape(ROWS, Y, X).astype(BF16)

    for i in range(HALF):
        @pl.when(m != i)
        def _():
            pltpu.make_async_remote_copy(
                src_ref=wg_out.at[mine + i], dst_ref=wg_out.at[mine + i], send_sem=ag_send.at[0],
                recv_sem=ag_recv.at[i], device_id=xy_dev(i), device_id_type=MESH).wait_recv()
            forward(i).start()
    for i in range(HALF):
        pltpu.make_async_remote_copy(
            src_ref=wg_out.at[theirs + i], dst_ref=wg_out.at[theirs + i], send_sem=fwd_send.at[i],
            recv_sem=fwd_recv.at[i], device_id=(sibling, r), device_id_type=MESH).wait_recv()

    for d in range(1, ROT):
        rot_copy(d).wait_send()
    for side in range(2):
        halo_copy(side).wait_send()
        part_copy(side).wait_send()
    core_copy.wait_send()
    for i in range(HALF):
        forward(i).wait_send()

        @pl.when(m != i)
        def _():
            xy_copy(i).wait_send()

    @pl.when(m < HALF)
    def _():
        for d in range(1, 8):
            z_copy(d).wait_send()
        for d in range(1, 16):
            ag_copy(d).wait_send()


def local(features, cotangent, weight, relative, offset_perm):
    any_spec = pl.BlockSpec(memory_space=pl.ANY)
    smem = pl.BlockSpec(memory_space=pltpu.SMEM)
    vmem = pl.BlockSpec(memory_space=pltpu.VMEM)
    dma = pltpu.SemaphoreType.DMA
    fg, wg = pl.pallas_call(
        kernel,
        out_shape=(
            jax.ShapeDtypeStruct((ROWS, Y, X), BF16),
            jax.ShapeDtypeStruct((2 * HALF, G, C * C), F32),
        ),
        in_specs=[smem, smem, any_spec, any_spec, any_spec],
        out_specs=(vmem, vmem),
        scratch_shapes=[
            pltpu.VMEM((2, ROWS, Y, X), BF16),
            pltpu.VMEM((TAPS, G, C * C), BF16),
            pltpu.VMEM((ROWS * Y, X), F32),
            pltpu.VMEM((G, C, VOX), BF16),
            pltpu.VMEM((3 * LOCAL, C, VOX), BF16),
            pltpu.VMEM((LOCAL, TAPS * C, VOX), BF16),
            pltpu.VMEM((LOCAL, G * C, VOX), BF16),
            pltpu.VMEM((TAPS * G, C * C), F32),
            pltpu.VMEM((TAPS * G * C, X), F32),
            pltpu.VMEM((TAPS * G, C, X), BF16),
            pltpu.VMEM((TAPS * ROWS, G * C), BF16),
            pltpu.VMEM((LOCAL, TAPS, C, G * C), F32),
            pltpu.SMEM((LOCAL * G, 32), jnp.int32),
            pltpu.VMEM((2 * HALF, UNIT, X), F32),
            pltpu.VMEM((HALF, UNIT, X), F32),
            pltpu.VMEM((16, UNIT, X), F32),
            pltpu.VMEM((8, UNIT, X), F32),
            pltpu.VMEM((UNIT, X), F32),
            pltpu.VMEM((X, X), F32),
            pltpu.VMEM((9 * ROWS, VOX), F32),
            pltpu.VMEM((3, ROWS, VOX), F32),
            pltpu.VMEM((2, ROWS, VOX), F32),
            dma((3,)), dma((8,)), dma((8,)), dma((2,)), dma((2,)), dma, dma,
            dma((16,)), dma((16,)), dma((8,)), dma((8,)), dma((16,)), dma((16,)), dma((16,)), dma((16,)),
            dma((2,)), dma((2,)),
        ],
        compiler_params=pltpu.CompilerParams(
            collective_id=0, has_side_effects=True, vmem_limit_bytes=48 * 1024 * 1024
        ),
    )(
        relative, offset_perm,
        cotangent.reshape(ROWS, Y, X), features.reshape(ROWS, Y, X), weight,
    )
    return fg.reshape(features.shape), wg[:TAPS]


def solution(mesh):
    field = P("rot", None, "space", None, None)
    return jax.shard_map(
        local,
        mesh=mesh,
        in_specs=(field, field, P(), P(), P()),
        out_specs=(field, P()),
        check_vma=False,
    )
```

time: 423 us -> 62.7 us (0.15)
  waiting for transfers between devices: 262 us -> 0 us
  local copies, waits for them, and re-layouts: 73.1 us -> 5.69 us
  Pallas kernels: 0 us -> 56.1 us
  matrix products: 33.8 us -> 0 us
  blocking collectives: 25.1 us -> 0 us
  between operations: 16 us -> 0.65 us
  starting transfers between devices: 7.16 us -> 0 us
    psum x1 -> x0, waiting for transfers between devices: 262 us -> none  [local(): weight_total = lax.psum(weight_local, ('space', 'rot'))]
    pallas_call x0 -> x1, Pallas kernels: none -> 56.1 us  [local(): pl.pallas_call(kernel, out_shape=(jax.ShapeDtypeStruct((ROWS, Y, X), BF16...]
    another operation x55 -> x0, local copies, waits for them, and re-layouts: 50 us -> none  [gather_taps(): return jnp.stack(stacked, 0)]
    dot_general x6 -> x0, matrix products: 33.8 us -> none  [the longest x1 7.31 us: weight_terms(): jnp.einsum('hoq,ohkcj->qkcj', tap_table, by_label, precision=lax.Precisio...]
    all_gather x1 -> x0, blocking collectives: 25.1 us -> none  [local(): shard_piece = lax.all_gather(features, 'rot', axis=0, tiled=True)]
    concatenate x24 -> x0, local copies, waits for them, and re-layouts: 9.19 us -> none  [the longest x12 5.12 us: shift_axis(): return jnp.concatenate([kept_part, zero_plane], along_axis)]
    ppermute x2 -> x0, starting transfers between devices: 7.07 us -> none  [the longest x1 5.15 us: with_halo(): lax.ppermute(head, axis, [((i + 1) % count, i) for i in range(ends)])]
  transfers between devices with their start and end apart: 4 -> 0, of which waited for: 1 -> 0; matrix products, arithmetic and copies ran while one was open for 8% -> 0% of each run, Pallas kernels for 0% -> 0%
where the time goes in v1:
time: 62.7 us; the launch traced here: 62.5 us
  Pallas kernels  56.1 us (89%)
  local copies, waits for them, and re-layouts  5.69 us (9%)
  between operations  0.65 us (1%)
    pallas_call x1, Pallas kernels, local(): pl.pallas_call(kernel, out_shape=(jax.ShapeDtypeStruct((ROWS, Y, X), BF16...  56.1 us
    unnamed x11, local copies, waits for them, and re-layouts  4.8 us

profile of v1, /device:TPU:1, one launch (start us, length us, event | category | flops | bytes accessed | tf_op | source)
XLA Modules:
  0.0 62.5 jit_solution(6469161688735332359)
XLA Ops:
  0.6 0.0 copy-start
  0.6 1.0 %copy-done = bf16[27,24,256]{2,1,0:T(8,128)(2,1)S(1)} copy-done((bf16[27,24,256]{2,1,0:T(8,128)(2,1)S(1)}, bf16[27,24,256]{2,1,0:T(8,128)(2,1)}, u32[]{:S(2)}) %copy-start) | copy-done | bytes 331800
  1.6 0.0 copy-start.1
  1.6 0.9 %copy-done.1 = bf16[3,16,1,8,128]{4,3,2,1,0:T(8,128)(2,1)S(1)} copy-done((bf16[3,16,1,8,128]{4,3,2,1,0:T(8,128)(2,1)S(1)}, bf16[3,16,1,8,128]{4,3,2,1,0:T(8,128)(2,1)}, u32[]{:S(2)}) %copy-start.1) | copy-done | bytes 98328
  2.5 0.0 copy-start.2
  2.5 0.9 %copy-done.2 = bf16[3,16,1,8,128]{4,3,2,1,0:T(8,128)(2,1)S(1)} copy-done((bf16[3,16,1,8,128]{4,3,2,1,0:T(8,128)(2,1)S(1)}, bf16[3,16,1,8,128]{4,3,2,1,0:T(8,128)(2,1)}, u32[]{:S(2)}) %copy-start.2) | copy-done | bytes 98328
  3.4 0.0 copy-start.3
  3.4 0.7 %copy-done.3 = s32[24,24]{1,0:T(8,128)S(1)} copy-done((s32[24,24]{1,0:T(8,128)S(1)}, s32[24,24]{1,0:T(8,128)}, u32[]{:S(2)}) %copy-start.3) | copy-done | bytes 2328
  4.1 0.0 copy-start.4
  4.1 0.7 %copy-done.4 = s32[24,27]{1,0:T(8,128)S(1)} copy-done((s32[24,27]{1,0:T(8,128)S(1)}, s32[24,27]{1,0:T(8,128)}, u32[]{:S(2)}) %copy-start.4) | copy-done | bytes 2616
  4.8 56.1 %shard_map.68 = (bf16[48,8,128]{2,1,0:T(8,128)(2,1)S(1)}, f32[28,24,256]{2,1,0:T(8,128)S(1)}) custom-call(s32[24,24]{1,0:T(8,128)S(1)} %copy-done.3, s32[24,27]{1,0:T(8,128)S(1)} %copy-done.4, bf16[48,8,128]{2,1,0:T(8,128)(2,1)S(1)} %bitcast.6, bf16[48,8,128]{2,1,0:T(8,128)(2,1)S(1)} %bitcast.7, bf16[27,24,256]{2,1,0:T(8,128)(2,1)S(1)} %copy-done), custom_call_target="tpu_custom_call" | custom-call | tf_op jit(solution)/shard_map/pallas_call | solution.py:377
  61.0 0.9 %slice.3 = f32[27,24,256]{2,1,0:T(8,128)} slice(f32[28,24,256]{2,1,0:T(8,128)S(1)} %get-tuple-element.5), slice={[0:27], [0:24], [0:256]} | slice | bytes 1327104 | tf_op jit(solution)/shard_map/slice | solution.py:419
  61.8 0.6 %copy.9 = bf16[3,16,1,8,128]{4,3,2,1,0:T(8,128)(2,1)} copy(bf16[3,16,1,8,128]{4,3,2,1,0:T(8,128)(2,1)S(1)} %bitcast.5) | data formatting | bytes 196608
Async XLA Ops:
  0.6 1.0 %copy-start = (bf16[27,24,256]{2,1,0:T(8,128)(2,1)S(1)}, bf16[27,24,256]{2,1,0:T(8,128)(2,1)}, u32[]{:S(2)}) copy-start(bf16[27,24,256]{2,1,0:T(8,128)(2,1)} %w_in.1) | copy-start | bytes 995332
  1.6 0.9 %copy-start.1 = (bf16[3,16,1,8,128]{4,3,2,1,0:T(8,128)(2,1)S(1)}, bf16[3,16,1,8,128]{4,3,2,1,0:T(8,128)(2,1)}, u32[]{:S(2)}) copy-start(bf16[3,16,1,8,128]{4,3,2,1,0:T(8,128)(2,1)} %param.6) | copy-start | bytes 294916
  2.5 0.9 %copy-start.2 = (bf16[3,16,1,8,128]{4,3,2,1,0:T(8,128)(2,1)S(1)}, bf16[3,16,1,8,128]{4,3,2,1,0:T(8,128)(2,1)}, u32[]{:S(2)}) copy-start(bf16[3,16,1,8,128]{4,3,2,1,0:T(8,128)(2,1)} %param.5) | copy-start | bytes 294916
  3.4 0.7 %copy-start.3 = (s32[24,24]{1,0:T(8,128)S(1)}, s32[24,24]{1,0:T(8,128)}, u32[]{:S(2)}) copy-start(s32[24,24]{1,0:T(8,128)} %rel.1) | copy-start | bytes 6916
  4.1 0.7 %copy-start.4 = (s32[24,27]{1,0:T(8,128)S(1)}, s32[24,27]{1,0:T(8,128)}, u32[]{:S(2)}) copy-start(s32[24,27]{1,0:T(8,128)} %perm.1) | copy-start | bytes 7780

commit v2 on v1

v2 whole, which is shorter than its diff:
```python
import functools
import math

import jax
import jax.numpy as jnp
from jax import lax
from jax.experimental import pallas as pl
from jax.experimental.pallas import tpu as pltpu
from jax.sharding import PartitionSpec as P

MESH = pl.DeviceIdType.MESH
F32 = jnp.float32
BF16 = jnp.bfloat16
G, C, TAPS, Y, X = 24, 16, 27, 8, 128
ROT, SPACE = 8, 32
LOCAL = G // ROT
ROWS = LOCAL * C
VOX = Y * X
HALF = 14
UNIT = 48


def lane_iota(rows):
    return lax.broadcasted_iota(jnp.int32, (rows, X), 1)


def kernel(rel_in, perm_in, cot_in, feat_in, w_in, fg_out, wg_out,
           rel, perm, stage, fg_stage, wgv, win, lay, cot, feats, f27, pc, w32, w16, wsrc32, wsrc, wmat, quad, table,
           give, keep, core_in, xy_in, z_in, unit, trans, fgm, part, part_in,
           in_sem, rot_send, rot_recv, halo_send, halo_recv, core_send, core_recv,
           xy_send, xy_recv, z_send, z_recv, ag_send, ag_recv, fwd_send, fwd_recv,
           pt_send, pt_recv, out_sem):
    s = lax.axis_index("space")
    r = lax.axis_index("rot")
    core = lax.rem(s, 2)
    yy = lax.rem(s // 2, 4)
    z_hi = s // 8
    xx = lax.rem(r, 4)
    z_lo = r // 4
    m = yy * 4 + xx
    zz = z_hi * 2 + z_lo
    up, down = lax.rem(s + 1, SPACE), lax.rem(s + SPACE - 1, SPACE)
    sibling = s + 1 - 2 * core

    def xy_dev(i):
        return ((z_hi * 4 + i // 4) * 2 + core, z_lo * 4 + lax.rem(i, 4))

    def z_dev(i):
        return (((i // 2) * 4 + yy) * 2 + core, lax.rem(i, 2) * 4 + xx)

    cot_copy = pltpu.make_async_copy(cot_in, stage.at[0], in_sem.at[0])
    feat_copy = pltpu.make_async_copy(feat_in, stage.at[1], in_sem.at[1])
    w_copy = pltpu.make_async_copy(w_in, win, in_sem.at[2])
    cot_copy.start()
    feat_copy.start()
    rel_copy = pltpu.make_async_copy(rel_in, rel, in_sem.at[3])
    perm_copy = pltpu.make_async_copy(perm_in, perm, in_sem.at[4])
    rel_copy.start()
    perm_copy.start()
    w_copy.start()
    barrier = pltpu.get_barrier_semaphore()
    for d in range(1, ROT):
        pl.semaphore_signal(barrier, inc=1, device_id=(s, lax.rem(r + d, ROT)), device_id_type=MESH)
        pl.semaphore_signal(barrier, inc=1, device_id=z_dev(lax.rem(zz + d, 8)), device_id_type=MESH)
    for d in range(1, 16):
        pl.semaphore_signal(barrier, inc=1, device_id=xy_dev(lax.rem(m + d, 16)), device_id_type=MESH)
    for other in (up, down):
        pl.semaphore_signal(barrier, inc=1, device_id=(other, r), device_id_type=MESH)

    def flatten_plane(index, dst, row):
        lay[...] = stage[index].astype(F32).reshape(ROWS * Y, X)
        for y in range(Y):
            column = lay[pl.ds(y, ROWS, stride=Y), :].astype(BF16)
            dst[pl.ds(row, LOCAL), :, y * X:(y + 1) * X] = column.reshape(LOCAL, C, X)

    own = r * LOCAL
    cot_copy.wait()
    flatten_plane(0, cot, own)
    feat_copy.wait()
    flatten_plane(1, feats, LOCAL)
    pl.semaphore_wait(barrier, 31)

    def rot_copy(d):
        peer = lax.rem(z_lo + d // 4, 2) * 4 + lax.rem(xx + d % 4, 4)
        return pltpu.make_async_remote_copy(
            src_ref=cot.at[pl.ds(own, LOCAL)], dst_ref=cot.at[pl.ds(own, LOCAL)],
            send_sem=rot_send, recv_sem=rot_recv, device_id=(s, peer), device_id_type=MESH)

    def whole(buffer, count, sent, got):
        some = buffer.at[pl.ds(0, count)]
        return pltpu.make_async_remote_copy(
            src_ref=some, dst_ref=some, send_sem=sent, recv_sem=got, device_id=(up, r), device_id_type=MESH)

    rot_all = whole(cot, G - LOCAL, rot_send, rot_recv)
    halo_all = whole(feats, 2 * LOCAL, halo_send, halo_recv)
    part_all = whole(part_in, 2, pt_send, pt_recv)

    def halo_copy(side):
        return pltpu.make_async_remote_copy(
            src_ref=feats.at[pl.ds(LOCAL, LOCAL)], dst_ref=feats.at[pl.ds(2 * LOCAL * side, LOCAL)],
            send_sem=halo_send, recv_sem=halo_recv,
            device_id=(up if side == 0 else down, r), device_id_type=MESH)

    for d in (6, 5, 7, 2, 4, 1, 3):
        rot_copy(d).start()
    for side in range(2):
        halo_copy(side).start()

    rel_copy.wait()
    perm_copy.wait()
    same = rel[0, 0]

    def fill_table(k, carry):
        for g in range(LOCAL):
            h = rel[rel[r * LOCAL + g, same], rel[k, same]]
            turned_back = rel[h, same]
            table[g * G + k, 28] = h
            for q in range(TAPS):
                table[g * G + k, q] = perm[turned_back, q]
            table[g * G + k, TAPS] = 0
        return carry

    lax.fori_loop(0, G, fill_table, 0)

    w_copy.wait()

    def widen(q, carry):
        w32[pl.ds(pl.multiple_of(q * G, 8), G), :] = win[q].astype(F32)
        return carry

    lax.fori_loop(0, TAPS, widen, 0)
    w32[TAPS * G:, :] = jnp.zeros((8, C * C), F32)
    w16[...] = w32[...].astype(BF16)
    row_id = lax.broadcasted_iota(jnp.int32, (C * C, 2 * X), 0)
    col_id = lax.broadcasted_iota(jnp.int32, (C * C, 2 * X), 1)
    same_co = row_id // C == lax.rem(col_id, C)
    row_ci = lax.rem(row_id, C) - col_id // X

    def spread(step, carry):
        hot = jnp.where(jnp.logical_and(same_co, row_ci == 2 * step), 1.0, 0.0).astype(BF16)
        picked = jnp.dot(w16[...], hot, preferred_element_type=F32)
        for side in range(2):
            wsrc32[pl.ds(2 * step + side, TAPS * G, stride=C), :] = picked[:TAPS * G, side * X:(side + 1) * X]
        return carry

    lax.fori_loop(0, C // 2, spread, 0)

    def narrow(step, carry):
        rows = pl.ds(pl.multiple_of(step * G * C, 16), G * C)
        wsrc[pl.ds(step * G, G)] = wsrc32[rows, :].astype(BF16).reshape(G, C, X)
        return carry

    lax.fori_loop(0, TAPS, narrow, 0)
    group16 = lane_iota(C) // C

    halo_all.wait_recv()
    lane48 = lane_iota(ROWS)

    def fill_shifts(a, carry):
        inside = jnp.logical_and(jnp.logical_or(a != 0, s != 0), jnp.logical_or(a != 2, s != SPACE - 1))
        keep = jnp.where(inside, 1.0, 0.0).astype(F32)
        blank = jnp.zeros((C, X), BF16)
        for y in range(Y):
            plane = feats[pl.ds(a * LOCAL, LOCAL), :, y * X:(y + 1) * X].astype(F32).reshape(ROWS, X) * keep
            for c in range(3):
                if c == 0:
                    moved = jnp.where(lane48 == 0, 0.0, pltpu.roll(plane, 1, 1))
                elif c == 2:
                    moved = jnp.where(lane48 == X - 1, 0.0, pltpu.roll(plane, X - 1, 1))
                else:
                    moved = plane
                moved = moved.astype(BF16)
                for b in range(3):
                    target = y - (b - 1)
                    at = pl.multiple_of((a * 9 + b * 3 + c) * C, 16)
                    for g in range(LOCAL):
                        if 0 <= target < Y:
                            f27[g, pl.ds(at, C), target * X:(target + 1) * X] = moved[g * C:(g + 1) * C]
                        if (b == 2 and y == Y - 1) or (b == 0 and y == 0):
                            f27[g, pl.ds(at, C), y * X:(y + 1) * X] = blank
        return carry

    lax.fori_loop(0, 3, fill_shifts, 0)

    rot_all.wait_recv()

    def reorder(k, carry):
        for g in range(LOCAL):
            pc[g, pl.ds(pl.multiple_of(k * C, 16), C), :] = cot[table[g * G + k, 28]]
        return carry

    lax.fori_loop(0, G, reorder, 0)

    def pair_sums(g, carry):
        product = lax.dot_general(f27[g], pc[g], (((1,), (1,)), ((), ())), preferred_element_type=F32)
        for octet in range(3):
            quad[g, octet] = product[:, octet * X:(octet + 1) * X].reshape(TAPS, C, X)
        return carry

    lax.fori_loop(0, LOCAL, pair_sums, 0)

    def relabel(q):
        octets = []
        for octet in range(3):
            total = None
            for g in range(LOCAL):
                merged = None
                for j in range(8):
                    block = quad[g, octet, table[g * G + octet * 8 + j, q]]
                    merged = block if merged is None else jnp.where(group16 == j, block, merged)
                total = merged if total is None else total + merged
            octets.append(total)
        return octets

    mine = core * HALF
    theirs = HALF - mine

    def owner(step):
        row, column = 3 - step // 4, 3 - lax.rem(step, 4)
        dx = column + jnp.where(column == 3, -1, jnp.where(column == 2, 1, 0))
        dy = row + jnp.where(row == 3, -1, jnp.where(row == 2, 1, 0))
        return lax.rem(yy + dy, 4) * 4 + lax.rem(xx + dx, 4)

    def xy_copy(step):
        return pltpu.make_async_remote_copy(
            src_ref=keep.at[step], dst_ref=xy_in.at[m], send_sem=xy_send, recv_sem=xy_recv,
            device_id=xy_dev(owner(step)), device_id_type=MESH)

    def core_copy(chunk):
        return pltpu.make_async_remote_copy(
            src_ref=give.at[pl.ds(chunk * 4, 4)], dst_ref=core_in.at[pl.ds(chunk * 4, 4)],
            send_sem=core_send, recv_sem=core_recv.at[chunk],
            device_id=(sibling, r), device_id_type=MESH)

    def chunk_sums(chunk, first, dst):
        for step in range(chunk * 4, chunk * 4 + 4):
            octets = relabel(first + jnp.minimum(owner(step), HALF - 1))
            for octet in range(3):
                dst[step, octet * C:(octet + 1) * C, :] = octets[octet]

    def give_chunk(chunk):
        chunk_sums(chunk, theirs, give)
        core_copy(chunk).start()

    def keep_chunk(chunk):
        chunk_sums(chunk, mine, keep)
        core_copy(chunk).wait_recv()
        for step in range(chunk * 4, chunk * 4 + 4):
            keep[step] += core_in[step]
            if step < 15:
                @pl.when(owner(step) < HALF)
                def _():
                    xy_copy(step).start()

    give_chunk(0)
    give_chunk(1)
    keep_chunk(0)
    give_chunk(2)
    keep_chunk(1)
    give_chunk(3)
    keep_chunk(2)
    keep_chunk(3)

    def fill_filter(o, carry):
        for octet in range(3):
            turned = [perm[octet * 8 + j, o] * G for j in range(8)]
            for g in range(LOCAL):
                merged = None
                for j in range(8):
                    block = wsrc[turned[j] + rel[octet * 8 + j, r * LOCAL + g]]
                    merged = block if merged is None else jnp.where(group16 == j, block, merged)
                wmat[o, g * C:(g + 1) * C, octet * X:(octet + 1) * X] = merged
        return carry

    lax.fori_loop(0, TAPS, fill_filter, 0)

    def input_part(a):
        def product(n, carry):
            cols = pl.ds(pl.multiple_of(n * 256, 256), 256)
            fgm[:, cols] = jnp.dot(
                wmat[a * 9:(a + 1) * 9].reshape(9 * ROWS, G * C), cot[:, :, cols].reshape(G * C, 256), preferred_element_type=F32)
            return carry

        lax.fori_loop(0, VOX // 256, product, 0)
        for y in range(Y):
            total = None
            for c in range(3):
                column = None
                for b in range(3):
                    source = y - (b - 1)
                    if 0 <= source < Y:
                        term = fgm[(b * 3 + c) * ROWS:(b * 3 + c + 1) * ROWS, source * X:(source + 1) * X]
                        column = term if column is None else column + term
                if c == 0:
                    column = jnp.where(lane48 == X - 1, 0.0, pltpu.roll(column, X - 1, 1))
                elif c == 2:
                    column = jnp.where(lane48 == 0, 0.0, pltpu.roll(column, 1, 1))
                total = column if total is None else total + column
            part[a, :, y * X:(y + 1) * X] = total

    def part_copy(side):
        return pltpu.make_async_remote_copy(
            src_ref=part.at[2 - 2 * side], dst_ref=part_in.at[side], send_sem=pt_send,
            recv_sem=pt_recv, device_id=(up if side == 0 else down, r), device_id_type=MESH)

    def z_copy(d):
        peer = lax.rem(zz + d, 8)
        return pltpu.make_async_remote_copy(
            src_ref=unit, dst_ref=z_in.at[zz], send_sem=z_send, recv_sem=z_recv,
            device_id=z_dev(peer), device_id_type=MESH)

    @pl.when(m < HALF)
    def _():
        unit[...] = keep[15]
        whole(xy_in, 15, xy_send, xy_recv).wait_recv()
        for d in range(1, 16):
            unit[...] += xy_in[lax.rem(m + d, 16)]
        z_in[zz] = unit[...]
        for d in (4, 3, 5, 2, 6, 1, 7):
            z_copy(d).start()

    input_part(2)
    part_copy(0).start()
    input_part(0)
    part_copy(1).start()
    input_part(1)

    def ag_copy(d):
        return pltpu.make_async_remote_copy(
            src_ref=wgv.at[m], dst_ref=wgv.at[m], send_sem=ag_send, recv_sem=ag_recv.at[m],
            device_id=xy_dev(lax.rem(yy + d // 4, 4) * 4 + lax.rem(xx + d % 4, 4)), device_id_type=MESH)

    def forward(i):
        return pltpu.make_async_remote_copy(
            src_ref=wgv.at[i], dst_ref=wg_out.at[mine + i], send_sem=fwd_send, recv_sem=fwd_recv,
            device_id=(sibling, r), device_id_type=MESH)

    def write(i):
        return pltpu.make_async_copy(wgv.at[i], wg_out.at[mine + i], out_sem)

    @pl.when(m < HALF)
    def _():
        whole(z_in, 7, z_send, z_recv).wait_recv()
        total = z_in[0]
        for i in range(1, 8):
            total = total + z_in[i]
        blank = jnp.zeros((X - C, X), F32)
        for octet in range(3):
            trans[...] = jnp.concatenate([total[octet * C:(octet + 1) * C], blank], 0).T
            for side in range(2):
                joined = None
                for j in range(8):
                    rows = trans[pl.ds(side * 8 + j, 8, stride=C), :]
                    rows = rows if j == 0 else pltpu.roll(rows, j * C, 1)
                    joined = rows if joined is None else joined + rows
                wgv[m, octet * 8:(octet + 1) * 8, side * X:(side + 1) * X] = joined
        for d in (10, 9, 11, 6, 14, 5, 7, 13, 15, 8, 2, 1, 3, 4, 12):
            ag_copy(d).start()
        forward(m).start()
        write(m).start()

    part_all.wait_recv()
    low = jnp.where(s > 0, 1.0, 0.0).astype(F32)
    high = jnp.where(s < SPACE - 1, 1.0, 0.0).astype(F32)
    for y in range(Y):
        cols = slice(y * X, (y + 1) * X)
        lay[pl.ds(y, ROWS, stride=Y), :] = part[1, :, cols] + low * part_in[0, :, cols] + high * part_in[1, :, cols]
    fg_stage[...] = lay[...].reshape(ROWS, Y, X).astype(BF16)
    fg_copy = pltpu.make_async_copy(fg_stage, fg_out, in_sem.at[0])
    fg_copy.start()

    for i in range(HALF):
        @pl.when(m != i)
        def _():
            pltpu.make_async_remote_copy(
                src_ref=wgv.at[i], dst_ref=wgv.at[i], send_sem=ag_send,
                recv_sem=ag_recv.at[i], device_id=xy_dev(i), device_id_type=MESH).wait_recv()
            forward(i).start()
            write(i).start()

    forward_all = whole(wgv, HALF, fwd_send, fwd_recv)
    forward_all.wait_recv()

    rot_all.wait_send()
    halo_all.wait_send()
    part_all.wait_send()
    whole(give, 16, core_send, core_recv.at[0]).wait_send()
    forward_all.wait_send()
    pltpu.make_async_copy(wgv.at[pl.ds(0, HALF)], wg_out.at[pl.ds(0, HALF)], out_sem).wait()
    fg_copy.wait()

    @pl.when(m < HALF)
    def _():
        whole(keep, HALF - 1, xy_send, xy_recv).wait_send()
        whole(z_in, 7, z_send, z_recv).wait_send()
        whole(xy_in, 15, ag_send, ag_recv.at[0]).wait_send()

    @pl.when(m >= HALF)
    def _():
        whole(keep, HALF, xy_send, xy_recv).wait_send()


def local(features, cotangent, weight, relative, offset_perm):
    any_spec = pl.BlockSpec(memory_space=pl.ANY)
    dma = pltpu.SemaphoreType.DMA
    fg, wg = pl.pallas_call(
        kernel,
        out_shape=(
            jax.ShapeDtypeStruct((ROWS, Y, X), BF16),
            jax.ShapeDtypeStruct((2 * HALF, G, C * C), F32),
        ),
        in_specs=[any_spec] * 5,
        out_specs=(any_spec, any_spec),
        scratch_shapes=[
            pltpu.SMEM((G, G), jnp.int32),
            pltpu.SMEM((G, TAPS), jnp.int32),
            pltpu.VMEM((2, ROWS, Y, X), BF16),
            pltpu.VMEM((ROWS, Y, X), BF16),
            pltpu.VMEM((16, G, C * C), F32),
            pltpu.VMEM((TAPS, G, C * C), BF16),
            pltpu.VMEM((ROWS * Y, X), F32),
            pltpu.VMEM((G, C, VOX), BF16),
            pltpu.VMEM((3 * LOCAL, C, VOX), BF16),
            pltpu.VMEM((LOCAL, TAPS * C, VOX), BF16),
            pltpu.VMEM((LOCAL, G * C, VOX), BF16),
            pltpu.VMEM((656, C * C), F32),
            pltpu.VMEM((656, C * C), BF16),
            pltpu.VMEM((TAPS * G * C, X), F32),
            pltpu.VMEM((TAPS * G, C, X), BF16),
            pltpu.VMEM((TAPS, ROWS, G * C), BF16),
            pltpu.VMEM((LOCAL, 3, TAPS, C, X), F32),
            pltpu.SMEM((LOCAL * G, 32), jnp.int32),
            pltpu.VMEM((16, UNIT, X), F32),
            pltpu.VMEM((16, UNIT, X), F32),
            pltpu.VMEM((16, UNIT, X), F32),
            pltpu.VMEM((16, UNIT, X), F32),
            pltpu.VMEM((8, UNIT, X), F32),
            pltpu.VMEM((UNIT, X), F32),
            pltpu.VMEM((X, X), F32),
            pltpu.VMEM((9 * ROWS, VOX), F32),
            pltpu.VMEM((3, ROWS, VOX), F32),
            pltpu.VMEM((2, ROWS, VOX), F32),
            dma((5,)), dma, dma, dma, dma, dma, dma((4,)),
            dma, dma, dma, dma, dma, dma((16,)), dma, dma, dma, dma, dma,
        ],
        compiler_params=pltpu.CompilerParams(
            collective_id=0, has_side_effects=True, vmem_limit_bytes=63 * 1024 * 1024
        ),
    )(
        relative, offset_perm,
        cotangent.reshape(ROWS, Y, X), features.reshape(ROWS, Y, X), weight,
    )
    return fg.reshape(features.shape), wg[:TAPS] * (1.0 / math.sqrt(G * SPACE * VOX))


def solution(mesh):
    field = P("rot", None, "space", None, None)
    return jax.shard_map(
        local,
        mesh=mesh,
        in_specs=(field, field, P(), P(), P()),
        out_specs=(field, P()),
        check_vma=False,
    )
```

time: 62.7 us -> 53.2 us (0.85)
  Pallas kernels: 56.1 us -> 49.7 us
  local copies, waits for them, and re-layouts: 5.69 us -> 0.64 us
  other arithmetic: 0 us -> 2.02 us
    pallas_call x1, Pallas kernels: 56.1 us -> 49.7 us  [local(): pl.pallas_call(kernel, out_shape=(jax.ShapeDtypeStruct((ROWS, Y, X), BF16...]
    unnamed x11 -> x3, local copies, waits for them, and re-layouts: 4.8 us -> 0.64 us
    mul x0 -> x1, other arithmetic: none -> 2.02 us  [local(): wg[:TAPS] * (1.0 / math.sqrt(G * SPACE * VOX))]
    slice x1 -> x0, local copies, waits for them, and re-layouts: 0.88 us -> none  [local(): return (fg.reshape(features.shape), wg[:TAPS])]
where the time goes in v2:
time: 53.2 us; the launch traced here: 53 us
  Pallas kernels  49.7 us (93%)
  other arithmetic  2.02 us (4%)
  between operations  0.65 us (1%)
  local copies, waits for them, and re-layouts  0.64 us (1%)
    pallas_call x1, Pallas kernels, local(): pl.pallas_call(kernel, out_shape=(jax.ShapeDtypeStruct((ROWS, Y, X), BF16...  49.7 us
    mul x1, other arithmetic, local(): wg[:TAPS] * (1.0 / math.sqrt(G * SPACE * VOX))  2.02 us

profile of v2, /device:TPU:1, one launch (start us, length us, event | category | flops | bytes accessed | tf_op | source)
XLA Modules:
  0.0 53.0 jit_solution(15234201605156518562)
XLA Ops:
  0.6 49.7 %shard_map.68 = (bf16[48,8,128]{2,1,0:T(8,128)(2,1)}, f32[28,24,256]{2,1,0:T(8,128)}) custom-call(s32[24,24]{1,0:T(8,128)} %rel_in.1, s32[24,27]{1,0:T(8,128)} %perm_in.1, bf16[48,8,128]{2,1,0:T(8,128)(2,1)} %bitcast.6, bf16[48,8,128]{2,1,0:T(8,128)(2,1)} %bitcast.7, bf16[27,24,256]{2,1,0:T(8,128)(2,1)} %w_in.1), custom_call_target="tpu_custom_call" | custom-call | tf_op jit(solution)/shard_map/pallas_call | solution.py:406
  50.4 0.0 copy-start
  50.4 2.0 %slice_multiply_fusion = f32[27,24,256]{2,1,0:T(8,128)} fusion(f32[28,24,256]{2,1,0:T(8,128)} %get-tuple-element.5), kind=kLoop, calls=%fused_computation | loop fusion | flops 165888 | bytes 1327104 | tf_op jit(solution)/shard_map/mul | solution.py:453
  52.4 0.0 copy-done
  52.4 0.6 %copy.9 = bf16[3,16,1,8,128]{4,3,2,1,0:T(8,128)(2,1)} copy(bf16[3,16,1,8,128]{4,3,2,1,0:T(8,128)(2,1)S(1)} %bitcast.5) | data formatting | bytes 196608
Async XLA Ops:
  50.4 2.0 %copy-start = (bf16[48,8,128]{2,1,0:T(8,128)(2,1)S(1)}, bf16[48,8,128]{2,1,0:T(8,128)(2,1)}, u32[]{:S(2)}) copy-start(bf16[48,8,128]{2,1,0:T(8,128)(2,1)} %get-tuple-element.4) | copy-start | bytes 294916

commit v3 on v2

--- a/solution.py
+++ b/solution.py
@@ -25,11 +25,11 @@
 
 
 def kernel(rel_in, perm_in, cot_in, feat_in, w_in, fg_out, wg_out,
-           rel, perm, stage, fg_stage, wgv, win, lay, cot, feats, f27, pc, w32, w16, wsrc32, wsrc, wmat, quad, table,
+           rel, perm, stage, win, lay, cot, feats, f27, pc, w32, w16, wsrc, wmat, quad, table,
            give, keep, core_in, xy_in, z_in, unit, trans, fgm, part, part_in,
            in_sem, rot_send, rot_recv, halo_send, halo_recv, core_send, core_recv,
            xy_send, xy_recv, z_send, z_recv, ag_send, ag_recv, fwd_send, fwd_recv,
-           pt_send, pt_recv, out_sem):
+           pt_send, pt_recv):
     s = lax.axis_index("space")
     r = lax.axis_index("rot")
     core = lax.rem(s, 2)
@@ -37,13 +37,13 @@
     z_hi = s // 8
     xx = lax.rem(r, 4)
     z_lo = r // 4
-    m = yy * 4 + xx
+    m = lax.rem(yy * 4 + xx + 8, 16)
     zz = z_hi * 2 + z_lo
     up, down = lax.rem(s + 1, SPACE), lax.rem(s + SPACE - 1, SPACE)
     sibling = s + 1 - 2 * core
 
     def xy_dev(i):
-        return ((z_hi * 4 + i // 4) * 2 + core, z_lo * 4 + lax.rem(i, 4))
+        return ((z_hi * 4 + lax.rem(i // 4 + 2, 4)) * 2 + core, z_lo * 4 + lax.rem(i, 4))
 
     def z_dev(i):
         return (((i // 2) * 4 + yy) * 2 + core, lax.rem(i, 2) * 4 + xx)
@@ -92,8 +92,6 @@
             src_ref=some, dst_ref=some, send_sem=sent, recv_sem=got, device_id=(up, r), device_id_type=MESH)
 
     rot_all = whole(cot, G - LOCAL, rot_send, rot_recv)
-    halo_all = whole(feats, 2 * LOCAL, halo_send, halo_recv)
-    part_all = whole(part_in, 2, pt_send, pt_recv)
 
     def halo_copy(side):
         return pltpu.make_async_remote_copy(
@@ -101,10 +99,39 @@
             send_sem=halo_send, recv_sem=halo_recv,
             device_id=(up if side == 0 else down, r), device_id_type=MESH)
 
+    def each_side(act):
+        @pl.when(s < SPACE - 1)
+        def _():
+            act(0)
+
+        @pl.when(s > 0)
+        def _():
+            act(1)
+
+    def both_sides(buffer, size, sent, got, act):
+        inside = jnp.logical_and(s > 0, s < SPACE - 1)
+
+        @pl.when(inside)
+        def _():
+            act(whole(buffer, 2 * size, sent, got))
+
+        @pl.when(jnp.logical_not(inside))
+        def _():
+            act(whole(buffer, size, sent, got))
+
+    @pl.when(s == 0)
+    def _():
+        feats[0:LOCAL] = jnp.zeros((LOCAL, C, VOX), BF16)
+        part_in[0] = jnp.zeros((ROWS, VOX), F32)
+
+    @pl.when(s == SPACE - 1)
+    def _():
+        feats[2 * LOCAL:] = jnp.zeros((LOCAL, C, VOX), BF16)
+        part_in[1] = jnp.zeros((ROWS, VOX), F32)
+
+    each_side(lambda side: halo_copy(side).start())
     for d in (6, 5, 7, 2, 4, 1, 3):
         rot_copy(d).start()
-    for side in range(2):
-        halo_copy(side).start()
 
     rel_copy.wait()
     perm_copy.wait()
@@ -115,8 +142,10 @@
             h = rel[rel[r * LOCAL + g, same], rel[k, same]]
             turned_back = rel[h, same]
             table[g * G + k, 28] = h
-            for q in range(TAPS):
-                table[g * G + k, q] = perm[turned_back, q]
+            for q in range(HALF):
+                turned = perm[turned_back, q]
+                table[g * G + k, q] = turned
+                table[g * G + k, TAPS - 1 - q] = TAPS - 1 - turned
             table[g * G + k, TAPS] = 0
         return carry
 
@@ -136,32 +165,43 @@
     same_co = row_id // C == lax.rem(col_id, C)
     row_ci = lax.rem(row_id, C) - col_id // X
 
+    rows = wsrc.reshape(TAPS * G * C, X)
+
     def spread(step, carry):
         hot = jnp.where(jnp.logical_and(same_co, row_ci == 2 * step), 1.0, 0.0).astype(BF16)
         picked = jnp.dot(w16[...], hot, preferred_element_type=F32)
         for side in range(2):
-            wsrc32[pl.ds(2 * step + side, TAPS * G, stride=C), :] = picked[:TAPS * G, side * X:(side + 1) * X]
+            rows[pl.ds(2 * step + side, TAPS * G, stride=C), :] = picked[:TAPS * G, side * X:(side + 1) * X]
         return carry
 
     lax.fori_loop(0, C // 2, spread, 0)
 
-    def narrow(step, carry):
-        rows = pl.ds(pl.multiple_of(step * G * C, 16), G * C)
-        wsrc[pl.ds(step * G, G)] = wsrc32[rows, :].astype(BF16).reshape(G, C, X)
-        return carry
-
-    lax.fori_loop(0, TAPS, narrow, 0)
     group16 = lane_iota(C) // C
 
-    halo_all.wait_recv()
+    def fill_filter(o, carry):
+        for octet in range(3):
+            turned = [perm[octet * 8 + j, o] * G for j in range(8)]
+            for g in range(LOCAL):
+                merged, facing = None, None
+                for j in range(8):
+                    k = rel[octet * 8 + j, r * LOCAL + g]
+                    block = wsrc[turned[j] + k]
+                    merged = block if merged is None else jnp.where(group16 == j, block, merged)
+                    block = wsrc[(TAPS - 1) * G - turned[j] + k]
+                    facing = block if facing is None else jnp.where(group16 == j, block, facing)
+                wmat[o, g * C:(g + 1) * C, octet * X:(octet + 1) * X] = merged.astype(BF16)
+                wmat[TAPS - 1 - o, g * C:(g + 1) * C, octet * X:(octet + 1) * X] = facing.astype(BF16)
+        return carry
+
+    lax.fori_loop(0, HALF, fill_filter, 0)
+
+    both_sides(feats, LOCAL, halo_send, halo_recv, lambda copy: copy.wait_recv())
     lane48 = lane_iota(ROWS)
 
     def fill_shifts(a, carry):
-        inside = jnp.logical_and(jnp.logical_or(a != 0, s != 0), jnp.logical_or(a != 2, s != SPACE - 1))
-        keep = jnp.where(inside, 1.0, 0.0).astype(F32)
         blank = jnp.zeros((C, X), BF16)
         for y in range(Y):
-            plane = feats[pl.ds(a * LOCAL, LOCAL), :, y * X:(y + 1) * X].astype(F32).reshape(ROWS, X) * keep
+            plane = feats[pl.ds(a * LOCAL, LOCAL), :, y * X:(y + 1) * X].astype(F32).reshape(ROWS, X)
             for c in range(3):
                 if c == 0:
                     moved = jnp.where(lane48 == 0, 0.0, pltpu.roll(plane, 1, 1))
@@ -219,7 +259,7 @@
         row, column = 3 - step // 4, 3 - lax.rem(step, 4)
         dx = column + jnp.where(column == 3, -1, jnp.where(column == 2, 1, 0))
         dy = row + jnp.where(row == 3, -1, jnp.where(row == 2, 1, 0))
-        return lax.rem(yy + dy, 4) * 4 + lax.rem(xx + dx, 4)
+        return lax.rem(yy + dy + 2, 4) * 4 + lax.rem(xx + dx, 4)
 
     def xy_copy(step):
         return pltpu.make_async_remote_copy(
@@ -260,19 +300,6 @@
     give_chunk(3)
     keep_chunk(2)
     keep_chunk(3)
-
-    def fill_filter(o, carry):
-        for octet in range(3):
-            turned = [perm[octet * 8 + j, o] * G for j in range(8)]
-            for g in range(LOCAL):
-                merged = None
-                for j in range(8):
-                    block = wsrc[turned[j] + rel[octet * 8 + j, r * LOCAL + g]]
-                    merged = block if merged is None else jnp.where(group16 == j, block, merged)
-                wmat[o, g * C:(g + 1) * C, octet * X:(octet + 1) * X] = merged
-        return carry
-
-    lax.fori_loop(0, TAPS, fill_filter, 0)
 
     def input_part(a):
         def product(n, carry):
@@ -303,6 +330,20 @@
             src_ref=part.at[2 - 2 * side], dst_ref=part_in.at[side], send_sem=pt_send,
             recv_sem=pt_recv, device_id=(up if side == 0 else down, r), device_id_type=MESH)
 
+    def far(side):
+        return lax.rem(s, 8) == (7 if side == 0 else 0)
+
+    def send_part(side, when):
+        @pl.when(jnp.logical_and(when, s < SPACE - 1 if side == 0 else s > 0))
+        def _():
+            part_copy(side).start()
+
+    input_part(2)
+    send_part(0, jnp.logical_not(far(0)))
+    input_part(0)
+    send_part(1, jnp.logical_not(far(1)))
+    input_part(1)
+
     def z_copy(d):
         peer = lax.rem(zz + d, 8)
         return pltpu.make_async_remote_copy(
@@ -319,24 +360,21 @@
         for d in (4, 3, 5, 2, 6, 1, 7):
             z_copy(d).start()
 
-    input_part(2)
-    part_copy(0).start()
-    input_part(0)
-    part_copy(1).start()
-    input_part(1)
 
     def ag_copy(d):
         return pltpu.make_async_remote_copy(
-            src_ref=wgv.at[m], dst_ref=wgv.at[m], send_sem=ag_send, recv_sem=ag_recv.at[m],
-            device_id=xy_dev(lax.rem(yy + d // 4, 4) * 4 + lax.rem(xx + d % 4, 4)), device_id_type=MESH)
+            src_ref=wg_out.at[mine + m], dst_ref=wg_out.at[mine + m], send_sem=ag_send, recv_sem=ag_recv.at[m],
+            device_id=xy_dev(lax.rem(yy + d // 4 + 2, 4) * 4 + lax.rem(xx + d % 4, 4)), device_id_type=MESH)
+
+    def arrival(i):
+        return pltpu.make_async_remote_copy(
+            src_ref=wg_out.at[mine + i], dst_ref=wg_out.at[mine + i], send_sem=ag_send, recv_sem=ag_recv.at[i],
+            device_id=(up, r), device_id_type=MESH)
 
     def forward(i):
         return pltpu.make_async_remote_copy(
-            src_ref=wgv.at[i], dst_ref=wg_out.at[mine + i], send_sem=fwd_send, recv_sem=fwd_recv,
+            src_ref=wg_out.at[mine + i], dst_ref=wg_out.at[mine + i], send_sem=fwd_send, recv_sem=fwd_recv,
             device_id=(sibling, r), device_id_type=MESH)
-
-    def write(i):
-        return pltpu.make_async_copy(wgv.at[i], wg_out.at[mine + i], out_sem)
 
     @pl.when(m < HALF)
     def _():
@@ -344,6 +382,7 @@
         total = z_in[0]
         for i in range(1, 8):
             total = total + z_in[i]
+        total = total * (1.0 / math.sqrt(G * SPACE * VOX))
         blank = jnp.zeros((X - C, X), F32)
         for octet in range(3):
             trans[...] = jnp.concatenate([total[octet * C:(octet + 1) * C], blank], 0).T
@@ -353,41 +392,33 @@
                     rows = trans[pl.ds(side * 8 + j, 8, stride=C), :]
                     rows = rows if j == 0 else pltpu.roll(rows, j * C, 1)
                     joined = rows if joined is None else joined + rows
-                wgv[m, octet * 8:(octet + 1) * 8, side * X:(side + 1) * X] = joined
+                wg_out[mine + m, octet * 8:(octet + 1) * 8, side * X:(side + 1) * X] = joined
         for d in (10, 9, 11, 6, 14, 5, 7, 13, 15, 8, 2, 1, 3, 4, 12):
             ag_copy(d).start()
         forward(m).start()
-        write(m).start()
-
-    part_all.wait_recv()
-    low = jnp.where(s > 0, 1.0, 0.0).astype(F32)
-    high = jnp.where(s < SPACE - 1, 1.0, 0.0).astype(F32)
+
+    for side in range(2):
+        send_part(side, far(side))
+
+    both_sides(part_in, 1, pt_send, pt_recv, lambda copy: copy.wait_recv())
     for y in range(Y):
         cols = slice(y * X, (y + 1) * X)
-        lay[pl.ds(y, ROWS, stride=Y), :] = part[1, :, cols] + low * part_in[0, :, cols] + high * part_in[1, :, cols]
-    fg_stage[...] = lay[...].reshape(ROWS, Y, X).astype(BF16)
-    fg_copy = pltpu.make_async_copy(fg_stage, fg_out, in_sem.at[0])
-    fg_copy.start()
-
+        lay[pl.ds(y, ROWS, stride=Y), :] = part[1, :, cols] + part_in[0, :, cols] + part_in[1, :, cols]
+    fg_out[...] = lay[...].reshape(ROWS, Y, X).astype(BF16)
     for i in range(HALF):
         @pl.when(m != i)
         def _():
-            pltpu.make_async_remote_copy(
-                src_ref=wgv.at[i], dst_ref=wgv.at[i], send_sem=ag_send,
-                recv_sem=ag_recv.at[i], device_id=xy_dev(i), device_id_type=MESH).wait_recv()
+            arrival(i).wait_recv()
             forward(i).start()
-            write(i).start()
-
-    forward_all = whole(wgv, HALF, fwd_send, fwd_recv)
+
+    forward_all = whole(wg_out, HALF, fwd_send, fwd_recv)
     forward_all.wait_recv()
 
     rot_all.wait_send()
-    halo_all.wait_send()
-    part_all.wait_send()
+    both_sides(feats, LOCAL, halo_send, halo_recv, lambda copy: copy.wait_send())
+    both_sides(part_in, 1, pt_send, pt_recv, lambda copy: copy.wait_send())
     whole(give, 16, core_send, core_recv.at[0]).wait_send()
     forward_all.wait_send()
-    pltpu.make_async_copy(wgv.at[pl.ds(0, HALF)], wg_out.at[pl.ds(0, HALF)], out_sem).wait()
-    fg_copy.wait()
 
     @pl.when(m < HALF)
     def _():
@@ -400,23 +431,34 @@
         whole(keep, HALF, xy_send, xy_recv).wait_send()
 
 
+def finish(fg_in, wg_in, fg_out, wg_out, sem):
+    pieces = [pltpu.make_async_copy(fg_in, fg_out, sem.at[0])]
+    for i in range(3):
+        some = pl.ds(9 * i, 9)
+        pieces.append(pltpu.make_async_copy(wg_in.at[some], wg_out.at[some], sem.at[i + 1]))
+    for copy in pieces:
+        copy.start()
+    for copy in pieces:
+        copy.wait()
+
+
 def local(features, cotangent, weight, relative, offset_perm):
     any_spec = pl.BlockSpec(memory_space=pl.ANY)
+    vmem = pl.BlockSpec(memory_space=pltpu.VMEM)
+    hbm = functools.partial(pltpu.with_memory_space_constraint, memory_space=pltpu.HBM)
     dma = pltpu.SemaphoreType.DMA
     fg, wg = pl.pallas_call(
         kernel,
         out_shape=(
-            jax.ShapeDtypeStruct((ROWS, Y, X), BF16),
-            jax.ShapeDtypeStruct((2 * HALF, G, C * C), F32),
+            pltpu.VMEM((ROWS, Y, X), BF16),
+            pltpu.VMEM((2 * HALF, G, C * C), F32),
         ),
         in_specs=[any_spec] * 5,
-        out_specs=(any_spec, any_spec),
+        out_specs=(vmem, vmem),
         scratch_shapes=[
             pltpu.SMEM((G, G), jnp.int32),
             pltpu.SMEM((G, TAPS), jnp.int32),
             pltpu.VMEM((2, ROWS, Y, X), BF16),
-            pltpu.VMEM((ROWS, Y, X), BF16),
-            pltpu.VMEM((16, G, C * C), F32),
             pltpu.VMEM((TAPS, G, C * C), BF16),
             pltpu.VMEM((ROWS * Y, X), F32),
             pltpu.VMEM((G, C, VOX), BF16),
@@ -425,8 +467,7 @@
             pltpu.VMEM((LOCAL, G * C, VOX), BF16),
             pltpu.VMEM((656, C * C), F32),
             pltpu.VMEM((656, C * C), BF16),
-            pltpu.VMEM((TAPS * G * C, X), F32),
-            pltpu.VMEM((TAPS * G, C, X), BF16),
+            pltpu.VMEM((TAPS * G, C, X), F32),
             pltpu.VMEM((TAPS, ROWS, G * C), BF16),
             pltpu.VMEM((LOCAL, 3, TAPS, C, X), F32),
             pltpu.SMEM((LOCAL * G, 32), jnp.int32),
@@ -441,16 +482,27 @@
             pltpu.VMEM((3, ROWS, VOX), F32),
             pltpu.VMEM((2, ROWS, VOX), F32),
             dma((5,)), dma, dma, dma, dma, dma, dma((4,)),
-            dma, dma, dma, dma, dma, dma((16,)), dma, dma, dma, dma, dma,
+            dma, dma, dma, dma, dma, dma((16,)), dma, dma, dma, dma,
         ],
         compiler_params=pltpu.CompilerParams(
-            collective_id=0, has_side_effects=True, vmem_limit_bytes=63 * 1024 * 1024
+            collective_id=0, has_side_effects=True, vmem_limit_bytes=48 * 1024 * 1024
         ),
     )(
-        relative, offset_perm,
-        cotangent.reshape(ROWS, Y, X), features.reshape(ROWS, Y, X), weight,
+        hbm(relative), hbm(offset_perm),
+        hbm(cotangent.reshape(ROWS, Y, X)), hbm(features.reshape(ROWS, Y, X)), hbm(weight),
     )
-    return fg.reshape(features.shape), wg[:TAPS] * (1.0 / math.sqrt(G * SPACE * VOX))
+    fg, wg = pl.pallas_call(
+        finish,
+        out_shape=(
+            jax.ShapeDtypeStruct((ROWS, Y, X), BF16),
+            jax.ShapeDtypeStruct((TAPS, G, C * C), F32),
+        ),
+        in_specs=[vmem] * 2,
+        out_specs=(any_spec, any_spec),
+        scratch_shapes=[dma((4,))],
+        compiler_params=pltpu.CompilerParams(vmem_limit_bytes=8 * 1024 * 1024),
+    )(fg, wg)
+    return fg.reshape(features.shape), wg
 
 
 def solution(mesh):

time: 53.2 us -> 50 us (0.940)
  other arithmetic: 2.02 us -> 0 us
  Pallas kernels: 49.7 us -> 49 us
  local copies, waits for them, and re-layouts: 0.64 us -> 0 us
    mul x1 -> x0, other arithmetic: 2.02 us -> none  [local(): wg[:TAPS] * (1.0 / math.sqrt(G * SPACE * VOX))]
    pallas_call x1 -> x2, Pallas kernels: 49.7 us -> 49 us  [the longest x1 48.1 us: local(): pl.pallas_call(kernel, out_shape=(pltpu.VMEM((ROWS, Y, X), BF16), pltpu.V...]
    unnamed x3 -> x0, local copies, waits for them, and re-layouts: 0.64 us -> none
where the time goes in v3:
time: 50 us; the launch traced here: 49.7 us
  Pallas kernels  49 us (98%)
  between operations  0.64 us (1%)
    pallas_call x1, Pallas kernels, local(): pl.pallas_call(kernel, out_shape=(pltpu.VMEM((ROWS, Y, X), BF16), pltpu.V...  48.1 us

profile of v3, /device:TPU:1, one launch (start us, length us, event | category | flops | bytes accessed | tf_op | source)
XLA Modules:
  0.0 49.7 jit_solution(17113568155780972291)
XLA Ops:
  0.6 48.1 %shard_map.68 = (bf16[48,8,128]{2,1,0:T(8,128)(2,1)S(1)}, f32[28,24,256]{2,1,0:T(8,128)S(1)}) custom-call(s32[24,24]{1,0:T(8,128)} %rel_in.1, s32[24,27]{1,0:T(8,128)} %perm_in.1, bf16[48,8,128]{2,1,0:T(8,128)(2,1)} %bitcast.5, bf16[48,8,128]{2,1,0:T(8,128)(2,1)} %bitcast.6, bf16[27,24,256]{2,1,0:T(8,128)(2,1)} %w_in.1), custom_call_target="tpu_custom_call" | custom-call | tf_op jit(solution)/shard_map/pallas_call | solution.py:450
  48.8 0.9 %shard_map.69 = (bf16[48,8,128]{2,1,0:T(8,128)(2,1)}, f32[27,24,256]{2,1,0:T(8,128)}) custom-call(bf16[48,8,128]{2,1,0:T(8,128)(2,1)S(1)} %get-tuple-element.6.fg_in, f32[28,24,256]{2,1,0:T(8,128)S(1)} %get-tuple-element.7.wg_in), custom_call_target="tpu_custom_call" | custom-call | tf_op jit(solution)/shard_map/pallas_call | solution.py:494

commit v4 on v3

--- a/solution.py
+++ b/solution.py
@@ -24,9 +24,27 @@
     return lax.broadcasted_iota(jnp.int32, (rows, X), 1)
 
 
+def turn(blocks, flips, swap, once, twice):
+    def at(a, b, c):
+        return blocks[a * 9 + b * 3 + c]
+
+    digits = [(a, b, c) for a in range(3) for b in range(3) for c in range(3)]
+    for axis in range(3):
+        step = (9, 3, 1)[axis]
+        blocks = [
+            v if digits[o][axis] == 1 else jnp.where(flips[axis], blocks[o + 2 * step * (1 - digits[o][axis])], v)
+            for o, v in enumerate(blocks)
+        ]
+    blocks = [at(a, b, c) if a == b else jnp.where(swap, at(b, a, c), at(a, b, c)) for a, b, c in digits]
+    return [
+        at(a, b, c) if a == b == c else jnp.where(once, at(b, c, a), jnp.where(twice, at(c, a, b), at(a, b, c)))
+        for a, b, c in digits
+    ]
+
+
 def kernel(rel_in, perm_in, cot_in, feat_in, w_in, fg_out, wg_out,
-           rel, perm, stage, win, lay, cot, feats, f27, pc, w32, w16, wsrc, wmat, quad, table,
-           give, keep, core_in, xy_in, z_in, unit, trans, fgm, part, part_in,
+           rel, perm, stage, win, lay, cot_low, cot_high, feats, f27, pc, w32, w16, wsrc, wturn, wmat, quad, table, turns,
+           sums, core_in, xy_in, z_in, unit, trans, fgm, part, part_in,
            in_sem, rot_send, rot_recv, halo_send, halo_recv, core_send, core_recv,
            xy_send, xy_recv, z_send, z_recv, ag_send, ag_recv, fwd_send, fwd_recv,
            pt_send, pt_recv):
@@ -48,6 +66,17 @@
     def z_dev(i):
         return (((i // 2) * 4 + yy) * 2 + core, lax.rem(i, 2) * 4 + xx)
 
+    barrier = pltpu.get_barrier_semaphore()
+    for d in (4, 3, 5, 2, 6, 1, 7):
+        pl.semaphore_signal(barrier, inc=1, device_id=z_dev(lax.rem(zz + d, 8)), device_id_type=MESH)
+    for d in (10, 9, 11, 6, 14, 5, 7, 13, 15, 8, 2, 1, 3, 4, 12):
+        near = lax.rem(yy + d // 4 + 2, 4) * 4 + lax.rem(xx + d % 4, 4)
+        pl.semaphore_signal(barrier, inc=1, device_id=xy_dev(near), device_id_type=MESH)
+    for d in (6, 5, 7, 2, 4, 1, 3):
+        peer = lax.rem(z_lo + d // 4, 2) * 4 + lax.rem(xx + d % 4, 4)
+        pl.semaphore_signal(barrier, inc=1, device_id=(s, peer), device_id_type=MESH)
+    for other in (up, down):
+        pl.semaphore_signal(barrier, inc=1, device_id=(other, r), device_id_type=MESH)
     cot_copy = pltpu.make_async_copy(cot_in, stage.at[0], in_sem.at[0])
     feat_copy = pltpu.make_async_copy(feat_in, stage.at[1], in_sem.at[1])
     w_copy = pltpu.make_async_copy(w_in, win, in_sem.at[2])
@@ -58,40 +87,43 @@
     rel_copy.start()
     perm_copy.start()
     w_copy.start()
-    barrier = pltpu.get_barrier_semaphore()
-    for d in range(1, ROT):
-        pl.semaphore_signal(barrier, inc=1, device_id=(s, lax.rem(r + d, ROT)), device_id_type=MESH)
-        pl.semaphore_signal(barrier, inc=1, device_id=z_dev(lax.rem(zz + d, 8)), device_id_type=MESH)
-    for d in range(1, 16):
-        pl.semaphore_signal(barrier, inc=1, device_id=xy_dev(lax.rem(m + d, 16)), device_id_type=MESH)
-    for other in (up, down):
-        pl.semaphore_signal(barrier, inc=1, device_id=(other, r), device_id_type=MESH)
-
-    def flatten_plane(index, dst, row):
+    cot = (cot_low, cot_high)
+
+    def flatten_plane(index, place):
         lay[...] = stage[index].astype(F32).reshape(ROWS * Y, X)
         for y in range(Y):
             column = lay[pl.ds(y, ROWS, stride=Y), :].astype(BF16)
-            dst[pl.ds(row, LOCAL), :, y * X:(y + 1) * X] = column.reshape(LOCAL, C, X)
+            place(y, column.reshape(LOCAL, C, X))
 
     own = r * LOCAL
     cot_copy.wait()
-    flatten_plane(0, cot, own)
+
+    def place_cot(y, column):
+        at = y % 4 * X
+        cot[y // 4][pl.ds(own, LOCAL), :, at:at + X] = column
+
+    flatten_plane(0, place_cot)
     feat_copy.wait()
-    flatten_plane(1, feats, LOCAL)
+
+    def place_feats(y, column):
+        feats[LOCAL:2 * LOCAL, :, y * X:(y + 1) * X] = column
+
+    flatten_plane(1, place_feats)
     pl.semaphore_wait(barrier, 31)
 
-    def rot_copy(d):
+    def rot_copy(d, half):
         peer = lax.rem(z_lo + d // 4, 2) * 4 + lax.rem(xx + d % 4, 4)
-        return pltpu.make_async_remote_copy(
-            src_ref=cot.at[pl.ds(own, LOCAL)], dst_ref=cot.at[pl.ds(own, LOCAL)],
-            send_sem=rot_send, recv_sem=rot_recv, device_id=(s, peer), device_id_type=MESH)
+        block = cot[half].at[pl.ds(own, LOCAL)]
+        return pltpu.make_async_remote_copy(
+            src_ref=block, dst_ref=block, send_sem=rot_send, recv_sem=rot_recv.at[half],
+            device_id=(s, peer), device_id_type=MESH)
 
     def whole(buffer, count, sent, got):
         some = buffer.at[pl.ds(0, count)]
         return pltpu.make_async_remote_copy(
             src_ref=some, dst_ref=some, send_sem=sent, recv_sem=got, device_id=(up, r), device_id_type=MESH)
 
-    rot_all = whole(cot, G - LOCAL, rot_send, rot_recv)
+    rot_all = [whole(cot[half], G - LOCAL, rot_send, rot_recv.at[half]) for half in range(2)]
 
     def halo_copy(side):
         return pltpu.make_async_remote_copy(
@@ -130,26 +162,56 @@
         part_in[1] = jnp.zeros((ROWS, VOX), F32)
 
     each_side(lambda side: halo_copy(side).start())
-    for d in (6, 5, 7, 2, 4, 1, 3):
-        rot_copy(d).start()
+    for half in range(2):
+        for d in (6, 5, 7, 2, 4, 1, 3):
+            rot_copy(d, half).start()
 
     rel_copy.wait()
     perm_copy.wait()
     same = rel[0, 0]
 
-    def fill_table(k, carry):
-        for g in range(LOCAL):
-            h = rel[rel[r * LOCAL + g, same], rel[k, same]]
-            turned_back = rel[h, same]
-            table[g * G + k, 28] = h
-            for q in range(HALF):
-                turned = perm[turned_back, q]
-                table[g * G + k, q] = turned
-                table[g * G + k, TAPS - 1 - q] = TAPS - 1 - turned
-            table[g * G + k, TAPS] = 0
-        return carry
-
-    lax.fori_loop(0, G, fill_table, 0)
+    group8 = lane_iota(8) // C
+    basis = (22, 16, 14)
+
+    def keep_turn(slot, images):
+        sizes = [jnp.abs(v) for v in images]
+        once, twice = sizes[0] == 1, sizes[1] == 1
+        none = jnp.logical_not(jnp.logical_or(once, twice))
+        swap = jnp.logical_or(
+            jnp.logical_and(none, sizes[1] == 9),
+            jnp.logical_or(jnp.logical_and(once, sizes[2] == 9), jnp.logical_and(twice, sizes[0] == 9)))
+        lowest = [jnp.minimum(jnp.minimum(jnp.where(sizes[0] == n, images[0], n), jnp.where(sizes[1] == n, images[1], n)),
+                              jnp.where(sizes[2] == n, images[2], n)) < 0 for n in (9, 3, 1)]
+        for i, mask in enumerate((*lowest, swap, once, twice)):
+            turns[slot, i] = jnp.where(mask, 1, 0)
+
+    def turn_of(slot):
+        f0, f1, f2, swap, once, twice = [turns[slot, i] != 0 for i in range(6)]
+        return (f0, f1, f2), swap, once, twice
+
+    def fill_turns(slot, carry):
+        g, octet = slot // 3, lax.rem(slot, 3)
+        base = rel[r * LOCAL + g, same]
+        images = [jnp.zeros((8, X), jnp.int32) for _ in basis]
+        for j in range(8):
+            k = octet * 8 + j
+            h = rel[base, rel[k, same]]
+            back = rel[h, same]
+            table[g * G + k] = h
+            images = [jnp.where(group8 == j, perm[back, o] - 13, v) for v, o in zip(images, basis)]
+        keep_turn(slot, images)
+        return carry
+
+    lax.fori_loop(0, LOCAL * 3, fill_turns, 0)
+
+    def fill_own_turns(octet, carry):
+        images = [jnp.zeros((8, X), jnp.int32) for _ in basis]
+        for j in range(8):
+            images = [jnp.where(group8 == j, perm[octet * 8 + j, o] - 13, v) for v, o in zip(images, basis)]
+        keep_turn(LOCAL * 3 + octet, images)
+        return carry
+
+    lax.fori_loop(0, 3, fill_own_turns, 0)
 
     w_copy.wait()
 
@@ -176,24 +238,26 @@
 
     lax.fori_loop(0, C // 2, spread, 0)
 
-    group16 = lane_iota(C) // C
-
-    def fill_filter(o, carry):
-        for octet in range(3):
-            turned = [perm[octet * 8 + j, o] * G for j in range(8)]
-            for g in range(LOCAL):
-                merged, facing = None, None
+
+    def fill_filter(step, carry):
+        g, octet = step // 3, lax.rem(step, 3)
+        labels = [rel[octet * 8 + j, r * LOCAL + g] for j in range(8)]
+        turned = turn_of(LOCAL * 3 + octet)
+        lanes = pl.ds(pl.multiple_of(octet * X, X), X)
+        for part_of in range(2):
+            blocks = []
+            for q in range(TAPS):
+                merged = None
                 for j in range(8):
-                    k = rel[octet * 8 + j, r * LOCAL + g]
-                    block = wsrc[turned[j] + k]
-                    merged = block if merged is None else jnp.where(group16 == j, block, merged)
-                    block = wsrc[(TAPS - 1) * G - turned[j] + k]
-                    facing = block if facing is None else jnp.where(group16 == j, block, facing)
-                wmat[o, g * C:(g + 1) * C, octet * X:(octet + 1) * X] = merged.astype(BF16)
-                wmat[TAPS - 1 - o, g * C:(g + 1) * C, octet * X:(octet + 1) * X] = facing.astype(BF16)
-        return carry
-
-    lax.fori_loop(0, HALF, fill_filter, 0)
+                    block = wsrc[q, labels[j], 8 * part_of:8 * part_of + 8]
+                    merged = block if merged is None else jnp.where(group8 == j, block, merged)
+                blocks.append(merged)
+            at = pl.ds(pl.multiple_of(g * C + 8 * part_of, 8), 8)
+            for o, block in enumerate(turn(blocks, *turned)):
+                wturn[o, at, lanes] = block
+        return carry
+
+    lax.fori_loop(0, LOCAL * 3, fill_filter, 0)
 
     both_sides(feats, LOCAL, halo_send, halo_recv, lambda copy: copy.wait_recv())
     lane48 = lane_iota(ROWS)
@@ -222,93 +286,93 @@
 
     lax.fori_loop(0, 3, fill_shifts, 0)
 
-    rot_all.wait_recv()
-
-    def reorder(k, carry):
+    for half in range(2):
+        voxels = slice(half * VOX // 2, (half + 1) * VOX // 2)
+        rot_all[half].wait_recv()
+
+        def reorder(k, carry):
+            for g in range(LOCAL):
+                pc[g, pl.ds(pl.multiple_of(k * C, 16), C), voxels] = cot[half][table[g * G + k]]
+            return carry
+
+        lax.fori_loop(0, G, reorder, 0)
+
+        def pair_sums(g, carry):
+            product = lax.dot_general(
+                f27[g, :, voxels], pc[g, :, voxels], (((1,), (1,)), ((), ())), preferred_element_type=F32)
+            for octet in range(3):
+                some = product[:, octet * X:(octet + 1) * X].reshape(TAPS, C, X)
+                if half == 0:
+                    quad[g, octet] = some
+                else:
+                    quad[g, octet] += some
+            return carry
+
+        lax.fori_loop(0, LOCAL, pair_sums, 0)
+
+    def relabel(step, carry):
+        octet, part_of = step // 2, lax.rem(step, 2)
+        at = pl.ds(pl.multiple_of(octet * C + 8 * part_of, 8), 8)
+        half_at = pl.ds(pl.multiple_of(8 * part_of, 8), 8)
         for g in range(LOCAL):
-            pc[g, pl.ds(pl.multiple_of(k * C, 16), C), :] = cot[table[g * G + k, 28]]
-        return carry
-
-    lax.fori_loop(0, G, reorder, 0)
-
-    def pair_sums(g, carry):
-        product = lax.dot_general(f27[g], pc[g], (((1,), (1,)), ((), ())), preferred_element_type=F32)
-        for octet in range(3):
-            quad[g, octet] = product[:, octet * X:(octet + 1) * X].reshape(TAPS, C, X)
-        return carry
-
-    lax.fori_loop(0, LOCAL, pair_sums, 0)
-
-    def relabel(q):
-        octets = []
-        for octet in range(3):
-            total = None
-            for g in range(LOCAL):
-                merged = None
-                for j in range(8):
-                    block = quad[g, octet, table[g * G + octet * 8 + j, q]]
-                    merged = block if merged is None else jnp.where(group16 == j, block, merged)
-                total = merged if total is None else total + merged
-            octets.append(total)
-        return octets
+            turned = turn([quad[g, octet, o, half_at] for o in range(TAPS)], *turn_of(g * 3 + octet))
+            for q in range(TAPS):
+                if g == 0:
+                    sums[q // HALF, q % HALF, at] = turned[q]
+                else:
+                    sums[q // HALF, q % HALF, at] += turned[q]
+        return carry
+
+    sums[1, HALF - 1] = jnp.zeros((UNIT, X), F32)
+    for i in range(HALF, 16):
+        for half in range(2):
+            sums[half, i] = jnp.zeros((UNIT, X), F32)
+    lax.fori_loop(0, 6, relabel, 0)
 
     mine = core * HALF
-    theirs = HALF - mine
+
+    def row_of(chunk):
+        dy = (2, 3, 1, 0)[chunk]
+        return lax.rem(yy + dy + 2, 4)
 
     def owner(step):
-        row, column = 3 - step // 4, 3 - lax.rem(step, 4)
-        dx = column + jnp.where(column == 3, -1, jnp.where(column == 2, 1, 0))
-        dy = row + jnp.where(row == 3, -1, jnp.where(row == 2, 1, 0))
-        return lax.rem(yy + dy + 2, 4) * 4 + lax.rem(xx + dx, 4)
+        row, column = 3 - step // 4, 3 - step % 4
+        return row_of(step // 4) * 4 + lax.rem(xx + (2, 3, 1, 0)[step % 4], 4)
 
     def xy_copy(step):
         return pltpu.make_async_remote_copy(
-            src_ref=keep.at[step], dst_ref=xy_in.at[m], send_sem=xy_send, recv_sem=xy_recv,
+            src_ref=sums.at[core, owner(step)], dst_ref=xy_in.at[m], send_sem=xy_send, recv_sem=xy_recv,
             device_id=xy_dev(owner(step)), device_id_type=MESH)
 
     def core_copy(chunk):
         return pltpu.make_async_remote_copy(
-            src_ref=give.at[pl.ds(chunk * 4, 4)], dst_ref=core_in.at[pl.ds(chunk * 4, 4)],
+            src_ref=sums.at[1 - core, pl.ds(row_of(chunk) * 4, 4)], dst_ref=core_in.at[pl.ds(row_of(chunk) * 4, 4)],
             send_sem=core_send, recv_sem=core_recv.at[chunk],
             device_id=(sibling, r), device_id_type=MESH)
 
-    def chunk_sums(chunk, first, dst):
-        for step in range(chunk * 4, chunk * 4 + 4):
-            octets = relabel(first + jnp.minimum(owner(step), HALF - 1))
-            for octet in range(3):
-                dst[step, octet * C:(octet + 1) * C, :] = octets[octet]
-
-    def give_chunk(chunk):
-        chunk_sums(chunk, theirs, give)
+    for chunk in range(4):
         core_copy(chunk).start()
-
-    def keep_chunk(chunk):
-        chunk_sums(chunk, mine, keep)
+    for chunk in range(4):
         core_copy(chunk).wait_recv()
         for step in range(chunk * 4, chunk * 4 + 4):
-            keep[step] += core_in[step]
+            i = owner(step)
+            sums[core, i] += core_in[i]
             if step < 15:
-                @pl.when(owner(step) < HALF)
+                @pl.when(i < HALF)
                 def _():
                     xy_copy(step).start()
 
-    give_chunk(0)
-    give_chunk(1)
-    keep_chunk(0)
-    give_chunk(2)
-    keep_chunk(1)
-    give_chunk(3)
-    keep_chunk(2)
-    keep_chunk(3)
-
     def input_part(a):
-        def product(n, carry):
-            cols = pl.ds(pl.multiple_of(n * 256, 256), 256)
-            fgm[:, cols] = jnp.dot(
-                wmat[a * 9:(a + 1) * 9].reshape(9 * ROWS, G * C), cot[:, :, cols].reshape(G * C, 256), preferred_element_type=F32)
-            return carry
-
-        lax.fori_loop(0, VOX // 256, product, 0)
+        wmat[...] = wturn[pl.ds(a * 9, 9)].reshape(9 * ROWS, G * C).astype(BF16)
+
+        for half in range(2):
+            def product(n, carry):
+                cols = pl.ds(pl.multiple_of(n * 256, 256), 256)
+                fgm[half, :, cols] = jnp.dot(
+                    wmat[...], cot[half][:, :, cols].reshape(G * C, 256), preferred_element_type=F32)
+                return carry
+
+            lax.fori_loop(0, 2, product, 0)
         for y in range(Y):
             total = None
             for c in range(3):
@@ -316,7 +380,8 @@
                 for b in range(3):
                     source = y - (b - 1)
                     if 0 <= source < Y:
-                        term = fgm[(b * 3 + c) * ROWS:(b * 3 + c + 1) * ROWS, source * X:(source + 1) * X]
+                        at = source % 4 * X
+                        term = fgm[source // 4, (b * 3 + c) * ROWS:(b * 3 + c + 1) * ROWS, at:at + X]
                         column = term if column is None else column + term
                 if c == 0:
                     column = jnp.where(lane48 == X - 1, 0.0, pltpu.roll(column, X - 1, 1))
@@ -330,18 +395,27 @@
             src_ref=part.at[2 - 2 * side], dst_ref=part_in.at[side], send_sem=pt_send,
             recv_sem=pt_recv, device_id=(up if side == 0 else down, r), device_id_type=MESH)
 
-    def far(side):
-        return lax.rem(s, 8) == (7 if side == 0 else 0)
-
-    def send_part(side, when):
-        @pl.when(jnp.logical_and(when, s < SPACE - 1 if side == 0 else s > 0))
+    crosses_z = lax.rem(s, 8) == 7 * core
+
+    def send_part(side):
+        @pl.when(s < SPACE - 1 if side == 0 else s > 0)
         def _():
             part_copy(side).start()
 
-    input_part(2)
-    send_part(0, jnp.logical_not(far(0)))
-    input_part(0)
-    send_part(1, jnp.logical_not(far(1)))
+    def send_out(when):
+        for side in range(2):
+            @pl.when(jnp.logical_and(core == 1 - side, when))
+            def _():
+                send_part(side)
+
+    input_part(2 * core)
+    send_out(crosses_z)
+    input_part(2 - 2 * core)
+    for side in range(2):
+        @pl.when(core == side)
+        def _():
+            send_part(side)
+
     input_part(1)
 
     def z_copy(d):
@@ -352,7 +426,7 @@
 
     @pl.when(m < HALF)
     def _():
-        unit[...] = keep[15]
+        unit[...] = sums[core, m]
         whole(xy_in, 15, xy_send, xy_recv).wait_recv()
         for d in range(1, 16):
             unit[...] += xy_in[lax.rem(m + d, 16)]
@@ -360,6 +434,8 @@
         for d in (4, 3, 5, 2, 6, 1, 7):
             z_copy(d).start()
 
+
+    send_out(jnp.logical_not(crosses_z))
 
     def ag_copy(d):
         return pltpu.make_async_remote_copy(
@@ -397,9 +473,6 @@
             ag_copy(d).start()
         forward(m).start()
 
-    for side in range(2):
-        send_part(side, far(side))
-
     both_sides(part_in, 1, pt_send, pt_recv, lambda copy: copy.wait_recv())
     for y in range(Y):
         cols = slice(y * X, (y + 1) * X)
@@ -414,21 +487,22 @@
     forward_all = whole(wg_out, HALF, fwd_send, fwd_recv)
     forward_all.wait_recv()
 
-    rot_all.wait_send()
+    for half in range(2):
+        rot_all[half].wait_send()
     both_sides(feats, LOCAL, halo_send, halo_recv, lambda copy: copy.wait_send())
     both_sides(part_in, 1, pt_send, pt_recv, lambda copy: copy.wait_send())
-    whole(give, 16, core_send, core_recv.at[0]).wait_send()
+    whole(core_in, 16, core_send, core_recv.at[0]).wait_send()
     forward_all.wait_send()
 
     @pl.when(m < HALF)
     def _():
-        whole(keep, HALF - 1, xy_send, xy_recv).wait_send()
+        whole(core_in, HALF - 1, xy_send, xy_recv).wait_send()
         whole(z_in, 7, z_send, z_recv).wait_send()
         whole(xy_in, 15, ag_send, ag_recv.at[0]).wait_send()
 
     @pl.when(m >= HALF)
     def _():
-        whole(keep, HALF, xy_send, xy_recv).wait_send()
+        whole(core_in, HALF, xy_send, xy_recv).wait_send()
 
 
 def finish(fg_in, wg_in, fg_out, wg_out, sem):
@@ -461,27 +535,29 @@
             pltpu.VMEM((2, ROWS, Y, X), BF16),
             pltpu.VMEM((TAPS, G, C * C), BF16),
             pltpu.VMEM((ROWS * Y, X), F32),
-            pltpu.VMEM((G, C, VOX), BF16),
+            pltpu.VMEM((G, C, VOX // 2), BF16),
+            pltpu.VMEM((G, C, VOX // 2), BF16),
             pltpu.VMEM((3 * LOCAL, C, VOX), BF16),
             pltpu.VMEM((LOCAL, TAPS * C, VOX), BF16),
             pltpu.VMEM((LOCAL, G * C, VOX), BF16),
             pltpu.VMEM((656, C * C), F32),
             pltpu.VMEM((656, C * C), BF16),
-            pltpu.VMEM((TAPS * G, C, X), F32),
-            pltpu.VMEM((TAPS, ROWS, G * C), BF16),
+            pltpu.VMEM((TAPS, G, C, X), F32),
+            pltpu.VMEM((TAPS, ROWS, G * C), F32),
+            pltpu.VMEM((9 * ROWS, G * C), BF16),
             pltpu.VMEM((LOCAL, 3, TAPS, C, X), F32),
-            pltpu.SMEM((LOCAL * G, 32), jnp.int32),
-            pltpu.VMEM((16, UNIT, X), F32),
-            pltpu.VMEM((16, UNIT, X), F32),
+            pltpu.SMEM((LOCAL * G,), jnp.int32),
+            pltpu.VMEM((12, 6, 8, X), jnp.int32),
+            pltpu.VMEM((2, 16, UNIT, X), F32),
             pltpu.VMEM((16, UNIT, X), F32),
             pltpu.VMEM((16, UNIT, X), F32),
             pltpu.VMEM((8, UNIT, X), F32),
             pltpu.VMEM((UNIT, X), F32),
             pltpu.VMEM((X, X), F32),
-            pltpu.VMEM((9 * ROWS, VOX), F32),
+            pltpu.VMEM((2, 9 * ROWS, VOX // 2), F32),
             pltpu.VMEM((3, ROWS, VOX), F32),
             pltpu.VMEM((2, ROWS, VOX), F32),
-            dma((5,)), dma, dma, dma, dma, dma, dma((4,)),
+            dma((5,)), dma, dma((2,)), dma, dma, dma, dma((4,)),
             dma, dma, dma, dma, dma, dma((16,)), dma, dma, dma, dma,
         ],
         compiler_params=pltpu.CompilerParams(

time: 50 us -> 48.6 us (0.972)
  Pallas kernels: 49 us -> 47.9 us
    pallas_call x1, Pallas kernels: 48.1 us -> 47 us  [local(): pl.pallas_call(kernel, out_shape=(pltpu.VMEM((ROWS, Y, X), BF16), pltpu.V...]
where the time goes in v4:
time: 48.6 us; the launch traced here: 48.5 us
  Pallas kernels  47.9 us (99%)
  between operations  0.64 us (1%)
    pallas_call x1, Pallas kernels, local(): pl.pallas_call(kernel, out_shape=(pltpu.VMEM((ROWS, Y, X), BF16), pltpu.V...  47 us

profile of v4, /device:TPU:1, one launch (start us, length us, event | category | flops | bytes accessed | tf_op | source)
XLA Modules:
  0.0 48.5 jit_solution(1107425220643011230)
XLA Ops:
  0.6 47.0 %shard_map.68 = (bf16[48,8,128]{2,1,0:T(8,128)(2,1)S(1)}, f32[28,24,256]{2,1,0:T(8,128)S(1)}) custom-call(s32[24,24]{1,0:T(8,128)} %rel_in.1, s32[24,27]{1,0:T(8,128)} %perm_in.1, bf16[48,8,128]{2,1,0:T(8,128)(2,1)} %bitcast.5, bf16[48,8,128]{2,1,0:T(8,128)(2,1)} %bitcast.6, bf16[27,24,256]{2,1,0:T(8,128)(2,1)} %w_in.1), custom_call_target="tpu_custom_call" | custom-call | tf_op jit(solution)/shard_map/pallas_call | solution.py:524
  47.6 0.9 %shard_map.69 = (bf16[48,8,128]{2,1,0:T(8,128)(2,1)}, f32[27,24,256]{2,1,0:T(8,128)}) custom-call(bf16[48,8,128]{2,1,0:T(8,128)(2,1)S(1)} %get-tuple-element.6.fg_in, f32[28,24,256]{2,1,0:T(8,128)S(1)} %get-tuple-element.7.wg_in), custom_call_target="tpu_custom_call" | custom-call | tf_op jit(solution)/shard_map/pallas_call | solution.py:570

commit v5 on v4

--- a/solution.py
+++ b/solution.py
@@ -16,7 +16,8 @@
 LOCAL = G // ROT
 ROWS = LOCAL * C
 VOX = Y * X
-HALF = 14
+PARTS = ((0, 4), (4, 8))
+SHARES = (11, 16)
 UNIT = 48
 
 
@@ -43,11 +44,11 @@
 
 
 def kernel(rel_in, perm_in, cot_in, feat_in, w_in, fg_out, wg_out,
-           rel, perm, stage, win, lay, cot_low, cot_high, feats, f27, pc, w32, w16, wsrc, wturn, wmat, quad, table, turns,
-           sums, core_in, xy_in, z_in, unit, trans, fgm, part, part_in,
-           in_sem, rot_send, rot_recv, halo_send, halo_recv, core_send, core_recv,
+           rel, perm, stage, win, lay, cot_0, cot_1, feats, f27, pc, w32, w16, wsrc, wturn, wmat, quad, table, turns,
+           sums, core_in, xy_in, z_in, unit, trans, fgm, part, part_in, passing,
+           in_sem, rot_send, rot_recv, across_recv, halo_send, halo_recv, core_send, core_recv,
            xy_send, xy_recv, z_send, z_recv, ag_send, ag_recv, fwd_send, fwd_recv,
-           pt_send, pt_recv):
+           pt_send, pt_recv, pass_send, pass_recv):
     s = lax.axis_index("space")
     r = lax.axis_index("rot")
     core = lax.rem(s, 2)
@@ -77,6 +78,12 @@
         pl.semaphore_signal(barrier, inc=1, device_id=(s, peer), device_id_type=MESH)
     for other in (up, down):
         pl.semaphore_signal(barrier, inc=1, device_id=(other, r), device_id_type=MESH)
+    at_end = lax.rem(s, 8) == 7 * core
+
+    @pl.when(at_end)
+    def _():
+        pl.semaphore_signal(barrier, inc=1, device_id=(s + 7 - 14 * core, r), device_id_type=MESH)
+
     cot_copy = pltpu.make_async_copy(cot_in, stage.at[0], in_sem.at[0])
     feat_copy = pltpu.make_async_copy(feat_in, stage.at[1], in_sem.at[1])
     w_copy = pltpu.make_async_copy(w_in, win, in_sem.at[2])
@@ -87,7 +94,9 @@
     rel_copy.start()
     perm_copy.start()
     w_copy.start()
-    cot = (cot_low, cot_high)
+    cot = (cot_0, cot_1)
+    part_of_row = [n for n, (first, last) in enumerate(PARTS) for _ in range(first, last)]
+    parts = range(len(PARTS))
 
     def flatten_plane(index, place):
         lay[...] = stage[index].astype(F32).reshape(ROWS * Y, X)
@@ -99,8 +108,9 @@
     cot_copy.wait()
 
     def place_cot(y, column):
-        at = y % 4 * X
-        cot[y // 4][pl.ds(own, LOCAL), :, at:at + X] = column
+        n = part_of_row[y]
+        at = (y - PARTS[n][0]) * X
+        cot[n][pl.ds(own, LOCAL), :, at:at + X] = column
 
     flatten_plane(0, place_cot)
     feat_copy.wait()
@@ -109,21 +119,29 @@
         feats[LOCAL:2 * LOCAL, :, y * X:(y + 1) * X] = column
 
     flatten_plane(1, place_feats)
-    pl.semaphore_wait(barrier, 31)
-
-    def rot_copy(d, half):
-        peer = lax.rem(z_lo + d // 4, 2) * 4 + lax.rem(xx + d % 4, 4)
+    pl.semaphore_wait(barrier, jnp.where(at_end, 32, 31))
+
+    across = lax.rem(r + 4, ROT)
+
+    def across_copy(half):
         block = cot[half].at[pl.ds(own, LOCAL)]
         return pltpu.make_async_remote_copy(
+            src_ref=block, dst_ref=block, send_sem=rot_send, recv_sem=across_recv.at[half],
+            device_id=(s, across), device_id_type=MESH)
+
+    def rot_copy(owner_of, d, half):
+        block = cot[half].at[pl.ds(owner_of * LOCAL, LOCAL)]
+        return pltpu.make_async_remote_copy(
             src_ref=block, dst_ref=block, send_sem=rot_send, recv_sem=rot_recv.at[half],
-            device_id=(s, peer), device_id_type=MESH)
+            device_id=(s, z_lo * 4 + lax.rem(xx + d, 4)), device_id_type=MESH)
 
     def whole(buffer, count, sent, got):
         some = buffer.at[pl.ds(0, count)]
         return pltpu.make_async_remote_copy(
             src_ref=some, dst_ref=some, send_sem=sent, recv_sem=got, device_id=(up, r), device_id_type=MESH)
 
-    rot_all = [whole(cot[half], G - LOCAL, rot_send, rot_recv.at[half]) for half in range(2)]
+    rot_sent = [whole(cot[half], G - LOCAL, rot_send, rot_recv.at[half]) for half in parts]
+    rot_all = [whole(cot[half], G - 2 * LOCAL, rot_send, rot_recv.at[half]) for half in parts]
 
     def halo_copy(side):
         return pltpu.make_async_remote_copy(
@@ -162,9 +180,11 @@
         part_in[1] = jnp.zeros((ROWS, VOX), F32)
 
     each_side(lambda side: halo_copy(side).start())
-    for half in range(2):
-        for d in (6, 5, 7, 2, 4, 1, 3):
-            rot_copy(d, half).start()
+    for half in parts:
+        across_copy(half).start()
+    for half in parts:
+        for d in (2, 1, 3):
+            rot_copy(r, d, half).start()
 
     rel_copy.wait()
     perm_copy.wait()
@@ -238,6 +258,11 @@
 
     lax.fori_loop(0, C // 2, spread, 0)
 
+
+    for half in parts:
+        whole(cot[half], LOCAL, rot_send, across_recv.at[half]).wait_recv()
+        for d in (2, 1, 3):
+            rot_copy(across, d, half).start()
 
     def fill_filter(step, carry):
         g, octet = step // 3, lax.rem(step, 3)
@@ -286,8 +311,8 @@
 
     lax.fori_loop(0, 3, fill_shifts, 0)
 
-    for half in range(2):
-        voxels = slice(half * VOX // 2, (half + 1) * VOX // 2)
+    for half in parts:
+        voxels = slice(PARTS[half][0] * X, PARTS[half][1] * X)
         rot_all[half].wait_recv()
 
         def reorder(k, carry):
@@ -318,18 +343,24 @@
             turned = turn([quad[g, octet, o, half_at] for o in range(TAPS)], *turn_of(g * 3 + octet))
             for q in range(TAPS):
                 if g == 0:
-                    sums[q // HALF, q % HALF, at] = turned[q]
+                    sums[int(q >= SHARES[0]), q - SHARES[0] * int(q >= SHARES[0]), at] = turned[q]
                 else:
-                    sums[q // HALF, q % HALF, at] += turned[q]
+                    sums[int(q >= SHARES[0]), q - SHARES[0] * int(q >= SHARES[0]), at] += turned[q]
         return carry
 
-    sums[1, HALF - 1] = jnp.zeros((UNIT, X), F32)
-    for i in range(HALF, 16):
-        for half in range(2):
-            sums[half, i] = jnp.zeros((UNIT, X), F32)
+    for i in range(SHARES[0], 16):
+        sums[0, i] = jnp.zeros((UNIT, X), F32)
     lax.fori_loop(0, 6, relabel, 0)
 
-    mine = core * HALF
+    mine = core * SHARES[0]
+    share = SHARES[0] + core * (SHARES[1] - SHARES[0])
+
+    def by_core(act):
+        for side in range(2):
+            @pl.when(core == side)
+            def _():
+                act(SHARES[side])
+
 
     def row_of(chunk):
         dy = (2, 3, 1, 0)[chunk]
@@ -358,21 +389,18 @@
             i = owner(step)
             sums[core, i] += core_in[i]
             if step < 15:
-                @pl.when(i < HALF)
+                @pl.when(i < share)
                 def _():
                     xy_copy(step).start()
 
     def input_part(a):
         wmat[...] = wturn[pl.ds(a * 9, 9)].reshape(9 * ROWS, G * C).astype(BF16)
 
-        for half in range(2):
-            def product(n, carry):
-                cols = pl.ds(pl.multiple_of(n * 256, 256), 256)
-                fgm[half, :, cols] = jnp.dot(
-                    wmat[...], cot[half][:, :, cols].reshape(G * C, 256), preferred_element_type=F32)
-                return carry
-
-            lax.fori_loop(0, 2, product, 0)
+        for n in parts:
+            for at in range(0, (PARTS[n][1] - PARTS[n][0]) * X, 256):
+                first = PARTS[n][0] * X + at
+                fgm[:, first:first + 256] = jnp.dot(
+                    wmat[...], cot[n][:, :, at:at + 256].reshape(G * C, 256), preferred_element_type=F32)
         for y in range(Y):
             total = None
             for c in range(3):
@@ -380,8 +408,7 @@
                 for b in range(3):
                     source = y - (b - 1)
                     if 0 <= source < Y:
-                        at = source % 4 * X
-                        term = fgm[source // 4, (b * 3 + c) * ROWS:(b * 3 + c + 1) * ROWS, at:at + X]
+                        term = fgm[(b * 3 + c) * ROWS:(b * 3 + c + 1) * ROWS, source * X:(source + 1) * X]
                         column = term if column is None else column + term
                 if c == 0:
                     column = jnp.where(lane48 == X - 1, 0.0, pltpu.roll(column, X - 1, 1))
@@ -395,27 +422,33 @@
             src_ref=part.at[2 - 2 * side], dst_ref=part_in.at[side], send_sem=pt_send,
             recv_sem=pt_recv, device_id=(up if side == 0 else down, r), device_id_type=MESH)
 
-    crosses_z = lax.rem(s, 8) == 7 * core
-
-    def send_part(side):
-        @pl.when(s < SPACE - 1 if side == 0 else s > 0)
+    crosses_z = at_end
+    onward = s + 8 * (2 * core - 1)
+    behind = s - 8 * (2 * core - 1)
+    relays = jnp.logical_and(crosses_z, jnp.logical_and(behind >= 0, behind < SPACE))
+
+    def along_z():
+        return pltpu.make_async_remote_copy(
+            src_ref=part.at[2 * core], dst_ref=passing, send_sem=pt_send, recv_sem=pass_recv,
+            device_id=(onward, r), device_id_type=MESH)
+
+    def along_y():
+        return pltpu.make_async_remote_copy(
+            src_ref=passing, dst_ref=part_in.at[1 - core], send_sem=pass_send, recv_sem=pt_recv,
+            device_id=(s + 7 - 14 * core, r), device_id_type=MESH)
+
+    def send_part(side, when):
+        @pl.when(jnp.logical_and(s < SPACE - 1 if side == 0 else s > 0, when))
         def _():
             part_copy(side).start()
 
-    def send_out(when):
-        for side in range(2):
-            @pl.when(jnp.logical_and(core == 1 - side, when))
-            def _():
-                send_part(side)
-
     input_part(2 * core)
-    send_out(crosses_z)
+
+    @pl.when(jnp.logical_and(crosses_z, jnp.logical_and(onward >= 0, onward < SPACE)))
+    def _():
+        along_z().start()
+
     input_part(2 - 2 * core)
-    for side in range(2):
-        @pl.when(core == side)
-        def _():
-            send_part(side)
-
     input_part(1)
 
     def z_copy(d):
@@ -424,7 +457,7 @@
             src_ref=unit, dst_ref=z_in.at[zz], send_sem=z_send, recv_sem=z_recv,
             device_id=z_dev(peer), device_id_type=MESH)
 
-    @pl.when(m < HALF)
+    @pl.when(m < share)
     def _():
         unit[...] = sums[core, m]
         whole(xy_in, 15, xy_send, xy_recv).wait_recv()
@@ -435,7 +468,13 @@
             z_copy(d).start()
 
 
-    send_out(jnp.logical_not(crosses_z))
+    for side in range(2):
+        send_part(side, jnp.logical_not(jnp.logical_and(crosses_z, core == 1 - side)))
+
+    @pl.when(relays)
+    def _():
+        along_z().wait_recv()
+        along_y().start()
 
     def ag_copy(d):
         return pltpu.make_async_remote_copy(
@@ -452,7 +491,7 @@
             src_ref=wg_out.at[mine + i], dst_ref=wg_out.at[mine + i], send_sem=fwd_send, recv_sem=fwd_recv,
             device_id=(sibling, r), device_id_type=MESH)
 
-    @pl.when(m < HALF)
+    @pl.when(m < share)
     def _():
         whole(z_in, 7, z_send, z_recv).wait_recv()
         total = z_in[0]
@@ -478,31 +517,35 @@
         cols = slice(y * X, (y + 1) * X)
         lay[pl.ds(y, ROWS, stride=Y), :] = part[1, :, cols] + part_in[0, :, cols] + part_in[1, :, cols]
     fg_out[...] = lay[...].reshape(ROWS, Y, X).astype(BF16)
-    for i in range(HALF):
-        @pl.when(m != i)
+    for i in range(16):
+        @pl.when(jnp.logical_and(m != i, i < share))
         def _():
             arrival(i).wait_recv()
             forward(i).start()
 
-    forward_all = whole(wg_out, HALF, fwd_send, fwd_recv)
-    forward_all.wait_recv()
-
-    for half in range(2):
-        rot_all[half].wait_send()
+    by_core(lambda count: whole(wg_out, TAPS - count, fwd_send, fwd_recv).wait_recv())
+
+    for half in parts:
+        rot_sent[half].wait_send()
     both_sides(feats, LOCAL, halo_send, halo_recv, lambda copy: copy.wait_send())
     both_sides(part_in, 1, pt_send, pt_recv, lambda copy: copy.wait_send())
     whole(core_in, 16, core_send, core_recv.at[0]).wait_send()
-    forward_all.wait_send()
-
-    @pl.when(m < HALF)
-    def _():
-        whole(core_in, HALF - 1, xy_send, xy_recv).wait_send()
+    by_core(lambda count: whole(wg_out, count, fwd_send, fwd_recv).wait_send())
+
+    @pl.when(relays)
+    def _():
+        along_y().wait_send()
+
+
+    @pl.when(m < share)
+    def _():
+        by_core(lambda count: whole(core_in, count - 1, xy_send, xy_recv).wait_send())
         whole(z_in, 7, z_send, z_recv).wait_send()
         whole(xy_in, 15, ag_send, ag_recv.at[0]).wait_send()
 
-    @pl.when(m >= HALF)
-    def _():
-        whole(core_in, HALF, xy_send, xy_recv).wait_send()
+    @pl.when(m >= share)
+    def _():
+        by_core(lambda count: whole(core_in, count, xy_send, xy_recv).wait_send())
 
 
 def finish(fg_in, wg_in, fg_out, wg_out, sem):
@@ -525,7 +568,7 @@
         kernel,
         out_shape=(
             pltpu.VMEM((ROWS, Y, X), BF16),
-            pltpu.VMEM((2 * HALF, G, C * C), F32),
+            pltpu.VMEM((TAPS, G, C * C), F32),
         ),
         in_specs=[any_spec] * 5,
         out_specs=(vmem, vmem),
@@ -535,8 +578,7 @@
             pltpu.VMEM((2, ROWS, Y, X), BF16),
             pltpu.VMEM((TAPS, G, C * C), BF16),
             pltpu.VMEM((ROWS * Y, X), F32),
-            pltpu.VMEM((G, C, VOX // 2), BF16),
-            pltpu.VMEM((G, C, VOX // 2), BF16),
+            *[pltpu.VMEM((G, C, (last - first) * X), BF16) for first, last in PARTS],
             pltpu.VMEM((3 * LOCAL, C, VOX), BF16),
             pltpu.VMEM((LOCAL, TAPS * C, VOX), BF16),
             pltpu.VMEM((LOCAL, G * C, VOX), BF16),
@@ -554,11 +596,12 @@
             pltpu.VMEM((8, UNIT, X), F32),
             pltpu.VMEM((UNIT, X), F32),
             pltpu.VMEM((X, X), F32),
-            pltpu.VMEM((2, 9 * ROWS, VOX // 2), F32),
+            pltpu.VMEM((9 * ROWS, VOX), F32),
             pltpu.VMEM((3, ROWS, VOX), F32),
             pltpu.VMEM((2, ROWS, VOX), F32),
-            dma((5,)), dma, dma((2,)), dma, dma, dma, dma((4,)),
-            dma, dma, dma, dma, dma, dma((16,)), dma, dma, dma, dma,
+            pltpu.VMEM((ROWS, VOX), F32),
+            dma((5,)), dma, dma((2,)), dma((2,)), dma, dma, dma, dma((4,)),
+            dma, dma, dma, dma, dma, dma((16,)), dma, dma, dma, dma, dma, dma,
         ],
         compiler_params=pltpu.CompilerParams(
             collective_id=0, has_side_effects=True, vmem_limit_bytes=48 * 1024 * 1024

time: 48.6 us -> 47.7 us (0.981)
  Pallas kernels: 47.9 us -> 47 us
    pallas_call x1, Pallas kernels: 47 us -> 46.1 us  [local(): pl.pallas_call(kernel, out_shape=(pltpu.VMEM((ROWS, Y, X), BF16), pltpu.V...]
where the time goes in v5:
time: 47.7 us; the launch traced here: 47.6 us
  Pallas kernels  47 us (99%)
  between operations  0.64 us (1%)
    pallas_call x1, Pallas kernels, local(): pl.pallas_call(kernel, out_shape=(pltpu.VMEM((ROWS, Y, X), BF16), pltpu.V...  46.1 us

profile of v5, /device:TPU:1, one launch (start us, length us, event | category | flops | bytes accessed | tf_op | source)
XLA Modules:
  0.0 47.6 jit_solution(6810869966578262059)
XLA Ops:
  0.6 46.1 %shard_map.68 = (bf16[48,8,128]{2,1,0:T(8,128)(2,1)S(1)}, f32[27,24,256]{2,1,0:T(8,128)S(1)}) custom-call(s32[24,24]{1,0:T(8,128)} %rel_in.1, s32[24,27]{1,0:T(8,128)} %perm_in.1, bf16[48,8,128]{2,1,0:T(8,128)(2,1)} %bitcast.5, bf16[48,8,128]{2,1,0:T(8,128)(2,1)} %bitcast.6, bf16[27,24,256]{2,1,0:T(8,128)(2,1)} %w_in.1), custom_call_target="tpu_custom_call" | custom-call | tf_op jit(solution)/shard_map/pallas_call | solution.py:567
  46.7 0.9 %shard_map.69 = (bf16[48,8,128]{2,1,0:T(8,128)(2,1)}, f32[27,24,256]{2,1,0:T(8,128)}) custom-call(bf16[48,8,128]{2,1,0:T(8,128)(2,1)S(1)} %get-tuple-element.6.fg_in, f32[27,24,256]{2,1,0:T(8,128)S(1)} %get-tuple-element.7.wg_in), custom_call_target="tpu_custom_call" | custom-call | tf_op jit(solution)/shard_map/pallas_call | solution.py:613

commit v6 on v5

--- a/solution.py
+++ b/solution.py
@@ -18,6 +18,7 @@
 VOX = Y * X
 PARTS = ((0, 4), (4, 8))
 SHARES = (11, 16)
+CODED = 64
 UNIT = 48
 
 
@@ -43,9 +44,22 @@
     ]
 
 
+def to_steps(sums):
+    top = jnp.max(jnp.max(jnp.abs(sums), axis=0, keepdims=True), axis=1, keepdims=True)
+    power = jnp.ceil(jnp.log2(jnp.maximum(jnp.broadcast_to(top, (8, X)), 2.0**-110)))
+    steps = jnp.round(sums * jnp.concatenate([jnp.exp2(15.0 - power)] * (UNIT // 8), 0))
+    steps = jnp.minimum(jnp.maximum(steps, -32767.0), 32767.0)
+    return jnp.concatenate([steps, power, power], 0).astype(jnp.int32).astype(jnp.int16)
+
+
+def from_steps(coded):
+    wide = coded.astype(jnp.int32).astype(F32)
+    return wide[:UNIT] * jnp.concatenate([jnp.exp2(wide[UNIT:UNIT + 8] - 15.0)] * (UNIT // 8), 0)
+
+
 def kernel(rel_in, perm_in, cot_in, feat_in, w_in, fg_out, wg_out,
            rel, perm, stage, win, lay, cot_0, cot_1, feats, f27, pc, w32, w16, wsrc, wturn, wmat, quad, table, turns,
-           sums, core_in, xy_in, z_in, unit, trans, fgm, part, part_in, passing,
+           sums, core_in, xy_in, xy_out, z_in, unit, trans, coded, fgm, part, part_in, passing,
            in_sem, rot_send, rot_recv, across_recv, halo_send, halo_recv, core_send, core_recv,
            xy_send, xy_recv, z_send, z_recv, ag_send, ag_recv, fwd_send, fwd_recv,
            pt_send, pt_recv, pass_send, pass_recv):
@@ -249,6 +263,11 @@
 
     rows = wsrc.reshape(TAPS * G * C, X)
 
+    def pass_on(half):
+        whole(cot[half], LOCAL, rot_send, across_recv.at[half]).wait_recv()
+        for d in (2, 1, 3):
+            rot_copy(across, d, half).start()
+
     def spread(step, carry):
         hot = jnp.where(jnp.logical_and(same_co, row_ci == 2 * step), 1.0, 0.0).astype(BF16)
         picked = jnp.dot(w16[...], hot, preferred_element_type=F32)
@@ -256,13 +275,12 @@
             rows[pl.ds(2 * step + side, TAPS * G, stride=C), :] = picked[:TAPS * G, side * X:(side + 1) * X]
         return carry
 
-    lax.fori_loop(0, C // 2, spread, 0)
-
-
-    for half in parts:
-        whole(cot[half], LOCAL, rot_send, across_recv.at[half]).wait_recv()
-        for d in (2, 1, 3):
-            rot_copy(across, d, half).start()
+    lax.fori_loop(0, 4, spread, 0)
+    pass_on(0)
+    lax.fori_loop(4, 6, spread, 0)
+    pass_on(1)
+    lax.fori_loop(6, C // 2, spread, 0)
+
 
     def fill_filter(step, carry):
         g, octet = step // 3, lax.rem(step, 3)
@@ -372,7 +390,7 @@
 
     def xy_copy(step):
         return pltpu.make_async_remote_copy(
-            src_ref=sums.at[core, owner(step)], dst_ref=xy_in.at[m], send_sem=xy_send, recv_sem=xy_recv,
+            src_ref=xy_out.at[owner(step)], dst_ref=xy_in.at[m], send_sem=xy_send, recv_sem=xy_recv,
             device_id=xy_dev(owner(step)), device_id_type=MESH)
 
     def core_copy(chunk):
@@ -387,11 +405,12 @@
         core_copy(chunk).wait_recv()
         for step in range(chunk * 4, chunk * 4 + 4):
             i = owner(step)
-            sums[core, i] += core_in[i]
             if step < 15:
-                @pl.when(i < share)
-                def _():
-                    xy_copy(step).start()
+                xy_out[i] = to_steps(sums[core, i] + core_in[i])
+        for step in range(chunk * 4, min(chunk * 4 + 4, 15)):
+            @pl.when(owner(step) < share)
+            def _():
+                xy_copy(step).start()
 
     def input_part(a):
         wmat[...] = wturn[pl.ds(a * 9, 9)].reshape(9 * ROWS, G * C).astype(BF16)
@@ -454,16 +473,16 @@
     def z_copy(d):
         peer = lax.rem(zz + d, 8)
         return pltpu.make_async_remote_copy(
-            src_ref=unit, dst_ref=z_in.at[zz], send_sem=z_send, recv_sem=z_recv,
+            src_ref=z_in.at[zz], dst_ref=z_in.at[zz], send_sem=z_send, recv_sem=z_recv,
             device_id=z_dev(peer), device_id_type=MESH)
 
     @pl.when(m < share)
     def _():
-        unit[...] = sums[core, m]
+        unit[...] = sums[core, m] + core_in[m]
         whole(xy_in, 15, xy_send, xy_recv).wait_recv()
         for d in range(1, 16):
-            unit[...] += xy_in[lax.rem(m + d, 16)]
-        z_in[zz] = unit[...]
+            unit[...] += from_steps(xy_in[lax.rem(m + d, 16)])
+        z_in[zz] = to_steps(unit[...])
         for d in (4, 3, 5, 2, 6, 1, 7):
             z_copy(d).start()
 
@@ -478,27 +497,33 @@
 
     def ag_copy(d):
         return pltpu.make_async_remote_copy(
-            src_ref=wg_out.at[mine + m], dst_ref=wg_out.at[mine + m], send_sem=ag_send, recv_sem=ag_recv.at[m],
+            src_ref=coded.at[mine + m], dst_ref=coded.at[mine + m], send_sem=ag_send, recv_sem=ag_recv.at[m],
             device_id=xy_dev(lax.rem(yy + d // 4 + 2, 4) * 4 + lax.rem(xx + d % 4, 4)), device_id_type=MESH)
 
+    def finish_offset(q):
+        block = from_steps(coded[q])
+        wg_out[q, :, :X] = block[:G]
+        wg_out[q, :, X:] = block[G:]
+
     def arrival(i):
         return pltpu.make_async_remote_copy(
-            src_ref=wg_out.at[mine + i], dst_ref=wg_out.at[mine + i], send_sem=ag_send, recv_sem=ag_recv.at[i],
+            src_ref=coded.at[mine + i], dst_ref=coded.at[mine + i], send_sem=ag_send, recv_sem=ag_recv.at[i],
             device_id=(up, r), device_id_type=MESH)
 
     def forward(i):
         return pltpu.make_async_remote_copy(
-            src_ref=wg_out.at[mine + i], dst_ref=wg_out.at[mine + i], send_sem=fwd_send, recv_sem=fwd_recv,
+            src_ref=coded.at[mine + i], dst_ref=coded.at[mine + i], send_sem=fwd_send, recv_sem=fwd_recv,
             device_id=(sibling, r), device_id_type=MESH)
 
     @pl.when(m < share)
     def _():
         whole(z_in, 7, z_send, z_recv).wait_recv()
-        total = z_in[0]
+        total = from_steps(z_in[0])
         for i in range(1, 8):
-            total = total + z_in[i]
+            total = total + from_steps(z_in[i])
         total = total * (1.0 / math.sqrt(G * SPACE * VOX))
         blank = jnp.zeros((X - C, X), F32)
+        sides = [[], []]
         for octet in range(3):
             trans[...] = jnp.concatenate([total[octet * C:(octet + 1) * C], blank], 0).T
             for side in range(2):
@@ -507,7 +532,8 @@
                     rows = trans[pl.ds(side * 8 + j, 8, stride=C), :]
                     rows = rows if j == 0 else pltpu.roll(rows, j * C, 1)
                     joined = rows if joined is None else joined + rows
-                wg_out[mine + m, octet * 8:(octet + 1) * 8, side * X:(side + 1) * X] = joined
+                sides[side].append(joined)
+        coded[mine + m] = to_steps(jnp.concatenate(sides[0] + sides[1], 0))
         for d in (10, 9, 11, 6, 14, 5, 7, 13, 15, 8, 2, 1, 3, 4, 12):
             ag_copy(d).start()
         forward(m).start()
@@ -522,15 +548,31 @@
         def _():
             arrival(i).wait_recv()
             forward(i).start()
-
-    by_core(lambda count: whole(wg_out, TAPS - count, fwd_send, fwd_recv).wait_recv())
+            finish_offset(mine + i)
+
+    @pl.when(m < share)
+    def _():
+        finish_offset(mine + m)
+
+    by_core(lambda count: whole(coded, TAPS - count, fwd_send, fwd_recv).wait_recv())
+
+    @pl.when(core == 0)
+    def _():
+        for q in range(SHARES[0], TAPS):
+            finish_offset(q)
+
+    @pl.when(core == 1)
+    def _():
+        for q in range(SHARES[0]):
+            finish_offset(q)
+
 
     for half in parts:
         rot_sent[half].wait_send()
     both_sides(feats, LOCAL, halo_send, halo_recv, lambda copy: copy.wait_send())
     both_sides(part_in, 1, pt_send, pt_recv, lambda copy: copy.wait_send())
     whole(core_in, 16, core_send, core_recv.at[0]).wait_send()
-    by_core(lambda count: whole(wg_out, count, fwd_send, fwd_recv).wait_send())
+    by_core(lambda count: whole(coded, count, fwd_send, fwd_recv).wait_send())
 
     @pl.when(relays)
     def _():
@@ -539,13 +581,13 @@
 
     @pl.when(m < share)
     def _():
-        by_core(lambda count: whole(core_in, count - 1, xy_send, xy_recv).wait_send())
+        by_core(lambda count: whole(xy_in, count - 1, xy_send, xy_recv).wait_send())
         whole(z_in, 7, z_send, z_recv).wait_send()
         whole(xy_in, 15, ag_send, ag_recv.at[0]).wait_send()
 
     @pl.when(m >= share)
     def _():
-        by_core(lambda count: whole(core_in, count, xy_send, xy_recv).wait_send())
+        by_core(lambda count: whole(xy_in, count, xy_send, xy_recv).wait_send())
 
 
 def finish(fg_in, wg_in, fg_out, wg_out, sem):
@@ -592,10 +634,12 @@
             pltpu.VMEM((12, 6, 8, X), jnp.int32),
             pltpu.VMEM((2, 16, UNIT, X), F32),
             pltpu.VMEM((16, UNIT, X), F32),
-            pltpu.VMEM((16, UNIT, X), F32),
-            pltpu.VMEM((8, UNIT, X), F32),
+            pltpu.VMEM((16, CODED, X), jnp.int16),
+            pltpu.VMEM((16, CODED, X), jnp.int16),
+            pltpu.VMEM((8, CODED, X), jnp.int16),
             pltpu.VMEM((UNIT, X), F32),
             pltpu.VMEM((X, X), F32),
+            pltpu.VMEM((TAPS, CODED, X), jnp.int16),
             pltpu.VMEM((9 * ROWS, VOX), F32),
             pltpu.VMEM((3, ROWS, VOX), F32),
             pltpu.VMEM((2, ROWS, VOX), F32),

time: 47.7 us -> 45.4 us (0.952)
  Pallas kernels: 47 us -> 44.6 us
    pallas_call x1, Pallas kernels: 46.1 us -> 43.7 us  [local(): pl.pallas_call(kernel, out_shape=(pltpu.VMEM((ROWS, Y, X), BF16), pltpu.V...]
where the time goes in v6:
time: 45.4 us; the launch traced here: 45.3 us
  Pallas kernels  44.6 us (98%)
  between operations  0.64 us (1%)
    pallas_call x1, Pallas kernels, local(): pl.pallas_call(kernel, out_shape=(pltpu.VMEM((ROWS, Y, X), BF16), pltpu.V...  43.7 us

profile of v6, /device:TPU:1, one launch (start us, length us, event | category | flops | bytes accessed | tf_op | source)
XLA Modules:
  0.0 45.3 jit_solution(18080219938227678544)
XLA Ops:
  0.6 43.7 %shard_map.68 = (bf16[48,8,128]{2,1,0:T(8,128)(2,1)S(1)}, f32[27,24,256]{2,1,0:T(8,128)S(1)}) custom-call(s32[24,24]{1,0:T(8,128)} %rel_in.1, s32[24,27]{1,0:T(8,128)} %perm_in.1, bf16[48,8,128]{2,1,0:T(8,128)(2,1)} %bitcast.5, bf16[48,8,128]{2,1,0:T(8,128)(2,1)} %bitcast.6, bf16[27,24,256]{2,1,0:T(8,128)(2,1)} %w_in.1), custom_call_target="tpu_custom_call" | custom-call | tf_op jit(solution)/shard_map/pallas_call | solution.py:609
  44.4 0.9 %shard_map.69 = (bf16[48,8,128]{2,1,0:T(8,128)(2,1)}, f32[27,24,256]{2,1,0:T(8,128)}) custom-call(bf16[48,8,128]{2,1,0:T(8,128)(2,1)S(1)} %get-tuple-element.6.fg_in, f32[27,24,256]{2,1,0:T(8,128)S(1)} %get-tuple-element.7.wg_in), custom_call_target="tpu_custom_call" | custom-call | tf_op jit(solution)/shard_map/pallas_call | solution.py:657

commit v7 on v6

--- a/solution.py
+++ b/solution.py
@@ -333,14 +333,11 @@
         voxels = slice(PARTS[half][0] * X, PARTS[half][1] * X)
         rot_all[half].wait_recv()
 
-        def reorder(k, carry):
-            for g in range(LOCAL):
-                pc[g, pl.ds(pl.multiple_of(k * C, 16), C), voxels] = cot[half][table[g * G + k]]
-            return carry
-
-        lax.fori_loop(0, G, reorder, 0)
-
-        def pair_sums(g, carry):
+        for g in range(LOCAL):
+            for k in range(G):
+                pc[g, k * C:(k + 1) * C, voxels] = cot[half][table[g * G + k]]
+
+        for g in range(LOCAL):
             product = lax.dot_general(
                 f27[g, :, voxels], pc[g, :, voxels], (((1,), (1,)), ((), ())), preferred_element_type=F32)
             for octet in range(3):
@@ -349,14 +346,11 @@
                     quad[g, octet] = some
                 else:
                     quad[g, octet] += some
-            return carry
-
-        lax.fori_loop(0, LOCAL, pair_sums, 0)
-
-    def relabel(step, carry):
-        octet, part_of = step // 2, lax.rem(step, 2)
-        at = pl.ds(pl.multiple_of(octet * C + 8 * part_of, 8), 8)
-        half_at = pl.ds(pl.multiple_of(8 * part_of, 8), 8)
+
+    def relabel(step):
+        octet, part_of = step // 2, step % 2
+        at = pl.ds(octet * C + 8 * part_of, 8)
+        half_at = pl.ds(8 * part_of, 8)
         for g in range(LOCAL):
             turned = turn([quad[g, octet, o, half_at] for o in range(TAPS)], *turn_of(g * 3 + octet))
             for q in range(TAPS):
@@ -364,11 +358,11 @@
                     sums[int(q >= SHARES[0]), q - SHARES[0] * int(q >= SHARES[0]), at] = turned[q]
                 else:
                     sums[int(q >= SHARES[0]), q - SHARES[0] * int(q >= SHARES[0]), at] += turned[q]
-        return carry
 
     for i in range(SHARES[0], 16):
         sums[0, i] = jnp.zeros((UNIT, X), F32)
-    lax.fori_loop(0, 6, relabel, 0)
+    for step in range(6):
+        relabel(step)
 
     mine = core * SHARES[0]
     share = SHARES[0] + core * (SHARES[1] - SHARES[0])
@@ -467,7 +461,11 @@
     def _():
         along_z().start()
 
+    for side in range(2):
+        send_part(side, jnp.logical_and(jnp.logical_not(crosses_z), core == 1 - side))
     input_part(2 - 2 * core)
+    for side in range(2):
+        send_part(side, core == side)
     input_part(1)
 
     def z_copy(d):
@@ -486,9 +484,6 @@
         for d in (4, 3, 5, 2, 6, 1, 7):
             z_copy(d).start()
 
-
-    for side in range(2):
-        send_part(side, jnp.logical_not(jnp.logical_and(crosses_z, core == 1 - side)))
 
     @pl.when(relays)
     def _():
@@ -538,11 +533,6 @@
             ag_copy(d).start()
         forward(m).start()
 
-    both_sides(part_in, 1, pt_send, pt_recv, lambda copy: copy.wait_recv())
-    for y in range(Y):
-        cols = slice(y * X, (y + 1) * X)
-        lay[pl.ds(y, ROWS, stride=Y), :] = part[1, :, cols] + part_in[0, :, cols] + part_in[1, :, cols]
-    fg_out[...] = lay[...].reshape(ROWS, Y, X).astype(BF16)
     for i in range(16):
         @pl.when(jnp.logical_and(m != i, i < share))
         def _():
@@ -553,6 +543,12 @@
     @pl.when(m < share)
     def _():
         finish_offset(mine + m)
+
+    both_sides(part_in, 1, pt_send, pt_recv, lambda copy: copy.wait_recv())
+    for y in range(Y):
+        cols = slice(y * X, (y + 1) * X)
+        lay[pl.ds(y, ROWS, stride=Y), :] = part[1, :, cols] + part_in[0, :, cols] + part_in[1, :, cols]
+    fg_out[...] = lay[...].reshape(ROWS, Y, X).astype(BF16)
 
     by_core(lambda count: whole(coded, TAPS - count, fwd_send, fwd_recv).wait_recv())
 

time: 45.4 us -> 44.3 us (0.976)
  Pallas kernels: 44.6 us -> 43.6 us
    pallas_call x1, Pallas kernels: 43.7 us -> 42.7 us  [local(): pl.pallas_call(kernel, out_shape=(pltpu.VMEM((ROWS, Y, X), BF16), pltpu.V...]
where the time goes in v7:
time: 44.3 us; the launch traced here: 44.2 us
  Pallas kernels  43.6 us (98%)
  between operations  0.64 us (1%)
    pallas_call x1, Pallas kernels, local(): pl.pallas_call(kernel, out_shape=(pltpu.VMEM((ROWS, Y, X), BF16), pltpu.V...  42.7 us
    pallas_call x1, Pallas kernels, local(): pl.pallas_call(finish, out_shape=(jax.ShapeDtypeStruct((ROWS, Y, X), BF16...  0.9 us

profile of v7, /device:TPU:1, one launch (start us, length us, event | category | flops | bytes accessed | tf_op | source)
XLA Modules:
  0.0 44.2 jit_solution(18257506946212543319)
XLA Ops:
  0.6 42.7 %shard_map.68 = (bf16[48,8,128]{2,1,0:T(8,128)(2,1)S(1)}, f32[27,24,256]{2,1,0:T(8,128)S(1)}) custom-call(s32[24,24]{1,0:T(8,128)} %rel_in.1, s32[24,27]{1,0:T(8,128)} %perm_in.1, bf16[48,8,128]{2,1,0:T(8,128)(2,1)} %bitcast.5, bf16[48,8,128]{2,1,0:T(8,128)(2,1)} %bitcast.6, bf16[27,24,256]{2,1,0:T(8,128)(2,1)} %w_in.1), custom_call_target="tpu_custom_call" | custom-call | tf_op jit(solution)/shard_map/pallas_call | solution.py:605
  43.3 0.9 %shard_map.69 = (bf16[48,8,128]{2,1,0:T(8,128)(2,1)}, f32[27,24,256]{2,1,0:T(8,128)}) custom-call(bf16[48,8,128]{2,1,0:T(8,128)(2,1)S(1)} %get-tuple-element.6.fg_in, f32[27,24,256]{2,1,0:T(8,128)S(1)} %get-tuple-element.7.wg_in), custom_call_target="tpu_custom_call" | custom-call | tf_op jit(solution)/shard_map/pallas_call | solution.py:653

commit v8 on v7

--- a/solution.py
+++ b/solution.py
@@ -342,17 +342,14 @@
                 f27[g, :, voxels], pc[g, :, voxels], (((1,), (1,)), ((), ())), preferred_element_type=F32)
             for octet in range(3):
                 some = product[:, octet * X:(octet + 1) * X].reshape(TAPS, C, X)
-                if half == 0:
-                    quad[g, octet] = some
-                else:
-                    quad[g, octet] += some
+                quad[half, g, octet] = some
 
     def relabel(step):
         octet, part_of = step // 2, step % 2
         at = pl.ds(octet * C + 8 * part_of, 8)
         half_at = pl.ds(8 * part_of, 8)
         for g in range(LOCAL):
-            turned = turn([quad[g, octet, o, half_at] for o in range(TAPS)], *turn_of(g * 3 + octet))
+            turned = turn([quad[0, g, octet, o, half_at] + quad[1, g, octet, o, half_at] for o in range(TAPS)], *turn_of(g * 3 + octet))
             for q in range(TAPS):
                 if g == 0:
                     sums[int(q >= SHARES[0]), q - SHARES[0] * int(q >= SHARES[0]), at] = turned[q]
@@ -384,7 +381,7 @@
 
     def xy_copy(step):
         return pltpu.make_async_remote_copy(
-            src_ref=xy_out.at[owner(step)], dst_ref=xy_in.at[m], send_sem=xy_send, recv_sem=xy_recv,
+            src_ref=xy_out.at[owner(step)], dst_ref=xy_in.at[m], send_sem=xy_send, recv_sem=xy_recv.at[int(step >= 11)],
             device_id=xy_dev(owner(step)), device_id_type=MESH)
 
     def core_copy(chunk):
@@ -477,9 +474,11 @@
     @pl.when(m < share)
     def _():
         unit[...] = sums[core, m] + core_in[m]
-        whole(xy_in, 15, xy_send, xy_recv).wait_recv()
-        for d in range(1, 16):
-            unit[...] += from_steps(xy_in[lax.rem(m + d, 16)])
+        for first, last in ((0, 11), (11, 15)):
+            whole(xy_in, last - first, xy_send, xy_recv.at[int(first > 0)]).wait_recv()
+            for step in range(first, last):
+                dx, dy = (2, 3, 1, 0)[step % 4], (2, 3, 1, 0)[step // 4]
+                unit[...] += from_steps(xy_in[lax.rem(yy - dy + 6, 4) * 4 + lax.rem(xx - dx + 4, 4)])
         z_in[zz] = to_steps(unit[...])
         for d in (4, 3, 5, 2, 6, 1, 7):
             z_copy(d).start()
@@ -577,13 +576,13 @@
 
     @pl.when(m < share)
     def _():
-        by_core(lambda count: whole(xy_in, count - 1, xy_send, xy_recv).wait_send())
+        by_core(lambda count: whole(xy_in, count - 1, xy_send, xy_recv.at[0]).wait_send())
         whole(z_in, 7, z_send, z_recv).wait_send()
         whole(xy_in, 15, ag_send, ag_recv.at[0]).wait_send()
 
     @pl.when(m >= share)
     def _():
-        by_core(lambda count: whole(xy_in, count, xy_send, xy_recv).wait_send())
+        by_core(lambda count: whole(xy_in, count, xy_send, xy_recv.at[0]).wait_send())
 
 
 def finish(fg_in, wg_in, fg_out, wg_out, sem):
@@ -625,7 +624,7 @@
             pltpu.VMEM((TAPS, G, C, X), F32),
             pltpu.VMEM((TAPS, ROWS, G * C), F32),
             pltpu.VMEM((9 * ROWS, G * C), BF16),
-            pltpu.VMEM((LOCAL, 3, TAPS, C, X), F32),
+            pltpu.VMEM((2, LOCAL, 3, TAPS, C, X), F32),
             pltpu.SMEM((LOCAL * G,), jnp.int32),
             pltpu.VMEM((12, 6, 8, X), jnp.int32),
             pltpu.VMEM((2, 16, UNIT, X), F32),
@@ -641,7 +640,7 @@
             pltpu.VMEM((2, ROWS, VOX), F32),
             pltpu.VMEM((ROWS, VOX), F32),
             dma((5,)), dma, dma((2,)), dma((2,)), dma, dma, dma, dma((4,)),
-            dma, dma, dma, dma, dma, dma((16,)), dma, dma, dma, dma, dma, dma,
+            dma, dma((2,)), dma, dma, dma, dma((16,)), dma, dma, dma, dma, dma, dma,
         ],
         compiler_params=pltpu.CompilerParams(
             collective_id=0, has_side_effects=True, vmem_limit_bytes=48 * 1024 * 1024

time: 44.3 us -> 44.3 us (level)
  no operation moved by 1% of the time
where the time goes in v8:
time: 44.3 us; the launch traced here: 44.2 us
  Pallas kernels  43.6 us (98%)
  between operations  0.64 us (1%)
    pallas_call x1, Pallas kernels, local(): pl.pallas_call(kernel, out_shape=(pltpu.VMEM((ROWS, Y, X), BF16), pltpu.V...  42.7 us
    pallas_call x1, Pallas kernels, local(): pl.pallas_call(finish, out_shape=(jax.ShapeDtypeStruct((ROWS, Y, X), BF16...  0.9 us

profile of v8, /device:TPU:1, one launch (start us, length us, event | category | flops | bytes accessed | tf_op | source)
XLA Modules:
  0.0 44.2 jit_solution(3043821878089812101)
XLA Ops:
  0.6 42.7 %shard_map.68 = (bf16[48,8,128]{2,1,0:T(8,128)(2,1)S(1)}, f32[27,24,256]{2,1,0:T(8,128)S(1)}) custom-call(s32[24,24]{1,0:T(8,128)} %rel_in.1, s32[24,27]{1,0:T(8,128)} %perm_in.1, bf16[48,8,128]{2,1,0:T(8,128)(2,1)} %bitcast.5, bf16[48,8,128]{2,1,0:T(8,128)(2,1)} %bitcast.6, bf16[27,24,256]{2,1,0:T(8,128)(2,1)} %w_in.1), custom_call_target="tpu_custom_call" | custom-call | tf_op jit(solution)/shard_map/pallas_call | solution.py:604
  43.3 0.9 %shard_map.69 = (bf16[48,8,128]{2,1,0:T(8,128)(2,1)}, f32[27,24,256]{2,1,0:T(8,128)}) custom-call(bf16[48,8,128]{2,1,0:T(8,128)(2,1)S(1)} %get-tuple-element.6.fg_in, f32[27,24,256]{2,1,0:T(8,128)S(1)} %get-tuple-element.7.wg_in), custom_call_target="tpu_custom_call" | custom-call | tf_op jit(solution)/shard_map/pallas_call | solution.py:652

commit v9 on v7

--- a/solution.py
+++ b/solution.py
@@ -485,11 +485,6 @@
             z_copy(d).start()
 
 
-    @pl.when(relays)
-    def _():
-        along_z().wait_recv()
-        along_y().start()
-
     def ag_copy(d):
         return pltpu.make_async_remote_copy(
             src_ref=coded.at[mine + m], dst_ref=coded.at[mine + m], send_sem=ag_send, recv_sem=ag_recv.at[m],
@@ -532,6 +527,11 @@
         for d in (10, 9, 11, 6, 14, 5, 7, 13, 15, 8, 2, 1, 3, 4, 12):
             ag_copy(d).start()
         forward(m).start()
+
+    @pl.when(relays)
+    def _():
+        along_z().wait_recv()
+        along_y().start()
 
     for i in range(16):
         @pl.when(jnp.logical_and(m != i, i < share))

time: 44.3 us -> 44.3 us (level)
  no operation moved by 1% of the time
where the time goes in v9:
time: 44.3 us; the launch traced here: 44.2 us
  Pallas kernels  43.6 us (98%)
  between operations  0.64 us (1%)
    pallas_call x1, Pallas kernels, local(): pl.pallas_call(kernel, out_shape=(pltpu.VMEM((ROWS, Y, X), BF16), pltpu.V...  42.7 us
    pallas_call x1, Pallas kernels, local(): pl.pallas_call(finish, out_shape=(jax.ShapeDtypeStruct((ROWS, Y, X), BF16...  0.9 us

profile of v9, /device:TPU:1, one launch (start us, length us, event | category | flops | bytes accessed | tf_op | source)
XLA Modules:
  0.0 44.2 jit_solution(18199589284828018262)
XLA Ops:
  0.6 42.7 %shard_map.68 = (bf16[48,8,128]{2,1,0:T(8,128)(2,1)S(1)}, f32[27,24,256]{2,1,0:T(8,128)S(1)}) custom-call(s32[24,24]{1,0:T(8,128)} %rel_in.1, s32[24,27]{1,0:T(8,128)} %perm_in.1, bf16[48,8,128]{2,1,0:T(8,128)(2,1)} %bitcast.5, bf16[48,8,128]{2,1,0:T(8,128)(2,1)} %bitcast.6, bf16[27,24,256]{2,1,0:T(8,128)(2,1)} %w_in.1), custom_call_target="tpu_custom_call" | custom-call | tf_op jit(solution)/shard_map/pallas_call | solution.py:605
  43.3 0.9 %shard_map.69 = (bf16[48,8,128]{2,1,0:T(8,128)(2,1)}, f32[27,24,256]{2,1,0:T(8,128)}) custom-call(bf16[48,8,128]{2,1,0:T(8,128)(2,1)S(1)} %get-tuple-element.6.fg_in, f32[27,24,256]{2,1,0:T(8,128)S(1)} %get-tuple-element.7.wg_in), custom_call_target="tpu_custom_call" | custom-call | tf_op jit(solution)/shard_map/pallas_call | solution.py:653
